TPU v7x, 32 devices: a whole 2x2x4 slice. The times are simulated.
32 devices in a mesh: groups: 2 (over y), date: 4 (over z), tile: 4 (over x, core).
Axes of the slice: x: 2, y: 2, z: 4, core: 2. Of those that a mesh axis runs over, the one named last changes fastest.
Arguments:
- slc: float32 [24, 2, 128, 1024], P('date', None, 'groups', 'tile'), parts along dimension 2, may hold values from -4 to 4, as said below
- pairs: int32 [64, 2], replicated, may hold values from 0 to 23, as said below
Outputs:
- interferogram: float32 [2, 64, 64, 256], P(None, 'date', 'groups', 'tile'), parts along dimension 2
- coherence: float32 [64, 64, 256], P('date', 'groups', 'tile'), parts along dimension 1
There are 2 independent parts, one for each index of `groups`. A program takes and returns all parts, laid end to end along the dimension named above; an argument that names none is the same for every part. Nothing has to cross between parts.
Inputs may be any that keep to these rules, and one draw needn't show every extreme that they name: Every pair's first date is below its second. In each block of 16 rows (rows k * 16 to (k + 1) * 16 - 1), the distinct dates used that lie among the 6 dates j * 6 to (j + 1) * 6 - 1 number at most 2, for every j; this bound is reached in every block. How many pairs a date takes part in varies. `slc`: every pixel's modulus is at least 0.3.
All inputs are finite; a program needn't handle non-finite values.
Results may differ from a plain program's by a relative error of at most 0.000058.
Values sent between devices are 32-bit elements; how exact they have to be, the bound alone decides.
A program may use at most 128 MiB of HBM per device.

v0:
```python
import math

import jax
import jax.numpy as jnp
from jax import lax
from jax.sharding import PartitionSpec as P

REQ = 2
AZ = 2
RG = 4
PATCH = 32


HIGHEST = lax.Precision.HIGHEST


def padded_2(block, sides, width):
    for axis, dim in sides:
        count = lax.axis_size(axis)
        forward = [(i, i + 1) for i in range(count - 1)]
        backward = [(target, source) for source, target in forward]
        low = lax.ppermute(
            lax.slice_in_dim(block, block.shape[dim] - width, None, axis=dim), axis, forward
        )
        high = lax.ppermute(lax.slice_in_dim(block, 0, width, axis=dim), axis, backward)
        block = jnp.concatenate([low, block, high], axis=dim)
    return block


def dft_tables(length):
    index = jnp.arange(length, dtype=jnp.int32)
    turns = index[:, None] * index[None, :] % length
    angle = 2.0 * math.pi / length * turns.astype(jnp.float32)
    return (jnp.cos(angle), -jnp.sin(angle))


def circulant(length):
    index = jnp.arange(length, dtype=jnp.int32)
    apart = (index[:, None] - index[None, :]) % length
    return ((apart == 0) | (apart == 1) | (apart == length - 1)).astype(jnp.float32)


def block_tables(length, count):
    index = jnp.arange(length * count, dtype=jnp.int32)
    within = index % length
    same = index[:, None] // length == index[None, :] // length
    cosine, sine = dft_tables(length)
    box_small = circulant(length)
    block_cos = jnp.where(same, cosine[within][:, within], 0.0)
    block_sin = jnp.where(same, sine[within][:, within], 0.0)
    block_box = jnp.where(same, box_small[within][:, within], 0.0)
    return (block_cos, block_sin, block_box, same.astype(jnp.float32))


def rows_apply(table, field):
    return jnp.einsum("kr,prx->pkx", table, field, precision=HIGHEST)


def cols_apply(field, table):
    return jnp.matmul(field, table, precision=HIGHEST)


def filter_patches(padded, local_cols):
    half = PATCH // 2
    count = local_cols // half + 1
    span = count * PATCH
    wide = padded.shape[3]
    slot_cols = jnp.arange(span, dtype=jnp.int32)
    source_col = slot_cols // PATCH * half + slot_cols % PATCH
    extract = (jnp.arange(wide, dtype=jnp.int32)[:, None] == source_col[None, :]).astype(
        jnp.float32
    )
    patches = jnp.matmul(padded, extract, precision=HIGHEST)
    real_in = patches[0]
    imag_in = patches[1]
    row_cos, row_sin = dft_tables(PATCH)
    row_box = circulant(PATCH)
    col_cos, col_sin, col_box, col_same = block_tables(PATCH, count)
    part_real = rows_apply(row_cos, real_in) - rows_apply(row_sin, imag_in)
    part_imag = rows_apply(row_cos, imag_in) + rows_apply(row_sin, real_in)
    spec_real = cols_apply(part_real, col_cos) - cols_apply(part_imag, col_sin)
    spec_imag = cols_apply(part_real, col_sin) + cols_apply(part_imag, col_cos)
    power = spec_real * spec_real + spec_imag * spec_imag
    smooth = cols_apply(rows_apply(row_box, power), col_box) / 9.0
    level = cols_apply(jnp.sum(smooth, axis=1, keepdims=True), col_same) / (PATCH * PATCH)
    response = ((smooth + 0.1 * level) / (level + 1e-06)) ** 0.25
    scaled_real = spec_real * response
    scaled_imag = spec_imag * response
    back_real = rows_apply(row_cos, scaled_real) + rows_apply(row_sin, scaled_imag)
    back_imag = rows_apply(row_cos, scaled_imag) - rows_apply(row_sin, scaled_real)
    final_real = (cols_apply(back_real, col_cos) + cols_apply(back_imag, col_sin)) / (PATCH * PATCH)
    final_imag = (cols_apply(back_imag, col_cos) - cols_apply(back_real, col_sin)) / (PATCH * PATCH)
    weight = jnp.sin(math.pi * ((slot_cols % PATCH).astype(jnp.float32) + 0.5) / PATCH) ** 2
    target = jnp.arange(local_cols, dtype=jnp.int32)
    landing = source_col[:, None] - half == target[None, :]
    mixing = jnp.where(landing, weight[:, None], 0.0)
    out_real = cols_apply(final_real, mixing)
    out_imag = cols_apply(final_imag, mixing)
    return jnp.stack([out_real, out_imag], axis=0)


def look_mean(field, group_size, local_cols):
    return field.reshape(group_size, PATCH, AZ, local_cols, RG).mean(axis=(2, 4))


def local(slc, pairs):
    dates_here = slc.shape[0]
    row_count = slc.shape[2]
    col_count = slc.shape[3]
    local_cols = col_count // RG
    owners = lax.axis_size("date")
    my_index = lax.axis_index("date")
    pair_count = pairs.shape[0] // owners
    all_dates = owners * dates_here
    flat_tiles = slc.reshape(dates_here, 2 * row_count * col_count)
    blocks = pairs.reshape(owners, pair_count, 2)
    date_ids = jnp.arange(all_dates, dtype=jnp.int32)
    used = jnp.any(blocks[:, :, :, None] == date_ids, axis=(1, 2))
    used_grid = used.reshape(owners, owners, dates_here)
    rank_grid = jnp.cumsum(used_grid.astype(jnp.int32), axis=2) - 1
    slot_ids = jnp.arange(REQ, dtype=jnp.int32)
    matched = used_grid[:, :, None, :] & (rank_grid[:, :, None, :] == slot_ids[:, None])
    picked = jnp.sum(matched.astype(jnp.int32) * jnp.arange(dates_here, dtype=jnp.int32), axis=3)
    filled = jnp.any(matched, axis=3).astype(jnp.float32)
    recv_pick = lax.dynamic_index_in_dim(picked, my_index, 0, keepdims=False)
    recv_fill = lax.dynamic_index_in_dim(filled, my_index, 0, keepdims=False)
    empty = jnp.zeros((owners * REQ, flat_tiles.shape[1]), jnp.float32)
    carry = empty
    piece = lax.all_gather(flat_tiles, "date", axis=0, tiled=True)
    start = jnp.int32(0)
    for offset in range(piece.shape[0] // dates_here):
        source = start // dates_here + offset
        index_row = lax.dynamic_index_in_dim(recv_pick, source, 0, keepdims=False)
        keep_row = lax.dynamic_index_in_dim(recv_fill, source, 0, keepdims=False)
        tiles_here = lax.dynamic_slice_in_dim(piece, offset * dates_here, dates_here, 0)
        taken = tiles_here[index_row] * keep_row[:, None]
        carry = lax.dynamic_update_slice_in_dim(carry, taken, source * REQ, 0)
    received = carry
    my_ranks = lax.dynamic_index_in_dim(rank_grid, my_index, 0, keepdims=False)
    source_of = jnp.arange(owners, dtype=jnp.int32)[:, None] * REQ
    slot_of = (source_of + my_ranks).reshape(all_dates)
    own_pairs = lax.dynamic_slice_in_dim(pairs, my_index * pair_count, pair_count, 0)
    hit_table = own_pairs[:, :, None] == date_ids
    pair_slots = jnp.sum(jnp.where(hit_table, slot_of, 0), axis=2)
    group_size = 8
    slot_blocks = pair_slots.reshape(pair_count // group_size, group_size, 2)

    def look_block(block):
        first = received[block[:, 0]].reshape(group_size, 2, row_count, col_count)
        second = received[block[:, 1]].reshape(group_size, 2, row_count, col_count)
        real_prod = first[:, 0] * second[:, 0] + first[:, 1] * second[:, 1]
        imag_prod = first[:, 1] * second[:, 0] - first[:, 0] * second[:, 1]
        power_ref = look_mean(
            first[:, 0] * first[:, 0] + first[:, 1] * first[:, 1], group_size, local_cols
        )
        power_sec = look_mean(
            second[:, 0] * second[:, 0] + second[:, 1] * second[:, 1], group_size, local_cols
        )
        looked_real = look_mean(real_prod, group_size, local_cols)
        looked_imag = look_mean(imag_prod, group_size, local_cols)
        coherent = (looked_real * looked_real + looked_imag * looked_imag) / (power_ref * power_sec)
        return (looked_real, looked_imag, coherent)

    looked_real, looked_imag, coherent = lax.map(look_block, slot_blocks)
    looked = jnp.stack(
        [
            looked_real.reshape(pair_count, PATCH, local_cols),
            looked_imag.reshape(pair_count, PATCH, local_cols),
        ],
        axis=0,
    )
    padded = padded_2(looked, (("tile", 3),), PATCH // 2)
    interferogram = filter_patches(padded, local_cols)
    return (interferogram, coherent.reshape(pair_count, PATCH, local_cols))


def solution(mesh):
    placed = (P("date", None, "groups", "tile"), P())
    return jax.shard_map(
        local,
        mesh=mesh,
        in_specs=placed,
        out_specs=(P(None, "date", "groups", "tile"), P("date", "groups", "tile")),
        check_vma=False,
    )
```

profile of v0, /device:TPU:1, one launch (start us, length us, event | category | flops | bytes accessed | tf_op | source)
XLA Modules:
  0.0 319.7 jit_solution(17133991070370579420)
XLA Ops:
  7.2 2.4 reshape.498
  21.6 71.1 %all-gather.3.cloned.1.call-done = f32[4,6,32768]{2,1,0:T(8,128)} async-done(((f32[1,6,32768]{2,1,0:T(8,128)}), f32[4,6,32768]{2,1,0:T(8,128)}) %all-gather.3.cloned.1.call-update) | async-done | bytes 3145744 | tf_op jit(solution)/shard_map/all_gather | solution.py:129
  92.7 3.4 %slice_bitcast_fusion = (f32[6,32768]{1,0:T(8,128)S(1)}, f32[6,32768]{1,0:T(8,128)S(1)}, f32[6,32768]{1,0:T(8,128)}, f32[6,32768]{1,0:T(8,128)S(1)}) fusion(f32[4,6,32768]{2,1,0:T(8,128)} %all-gather.3.cloned.1.call-done), kind=kLoop, calls=%fused_computation.47 | loop fusion | bytes 6291456 | tf_op jit(solution)/shard_map/dynamic_slice | solution.py:135
  97.0 2.1 gather_fusion.3
  102.9 177.2 %while.14 = (s32[]{:T(128)}, f32[2,8,32,64]{3,2,1,0:T(8,128)}, f32[2,8,32,64]{3,2,1,0:T(8,128)}, f32[2,8,32,64]{3,2,1,0:T(8,128)}, s32[2,8,2]{1,0,2:T(2,128)S(1)...) while((s32[]{:T(128)}, f32[2,8,32,64]{3,2,1,0:T(8,128)}, f32[2,8,32,64]{3,2,1,0:T(8,128)}, ...), condition=%wide.region_10.11_spmd, body=%wide.region_5.10_spmd.sunk | while | flops 2213938 | bytes 21832740 | solution.py:164
  104.2 4.8 %copy.133 = f32[8,1,64,256]{0,3,2,1:T(8,128)} copy(f32[8,1,64,256]{3,0,2,1:T(8,128)S(1)} %get-tuple-element.167) | data formatting | bytes 1048576 | tf_op jit(solution)/shard_map/while
  110.8 5.6 %copy.134 = f32[8,1,64,256]{0,3,2,1:T(8,128)} copy(f32[8,1,64,256]{3,0,2,1:T(8,128)} %get-tuple-element.169) | data formatting | bytes 1048576 | tf_op jit(solution)/shard_map/while
  116.5 4.8 %copy.135 = f32[8,1,64,256]{0,3,2,1:T(8,128)} copy(f32[8,1,64,256]{3,0,2,1:T(8,128)S(1)} %get-tuple-element.170) | data formatting | bytes 1048576 | tf_op jit(solution)/shard_map/while
  121.3 4.8 %copy.136 = f32[8,1,64,256]{0,3,2,1:T(8,128)} copy(f32[8,1,64,256]{3,0,2,1:T(8,128)S(1)} %get-tuple-element.171) | data formatting | bytes 1048576 | tf_op jit(solution)/shard_map/while
  126.1 22.1 %multiply_subtract_fusion.2 = (f32[8,1,64,256]{0,3,2,1:T(8,128)}, f32[8,1,64,256]{0,3,2,1:T(8,128)}, f32[8,1,64,256]{0,3,2,1:T(8,128)}, f32[8,1,64,256]{0,3,2,1:T(8,128)}) fusion(f32[8,1,64,256]{0,3,2,1:T(8,128)} %copy.133, f32[8,1,64,256]{0,3,2,1:T(8,128)} %copy.134, f32[8,1,64,256]{0,3,2,1:T(8,128)} %copy.135, f32[8,1,64,256]{0,3,2,1:T(8,128)} %copy.136), kind=kLoop, calls=%fused_computation.14.clone.1 | loop fusion | flops 1572864 | bytes 4194304 | tf_op jit(solution)/shard_map/while/body/eval_jaxpr/sub | solution.py:152
  148.1 6.8 %reduce_sum.73 = f32[8,32,64]{0,2,1:T(8,128)S(1)} reduce(f32[8,32,2,64,4]{0,4,3,2,1:T(4,128)} %bitcast.193, f32[]{:T(128)} %constant.379.clone.1..sunk), dimensions={2,4}, to_apply=%region_6.6 | reduce | flops 114688 | bytes 589828 | tf_op jit(solution)/shard_map/while/body/eval_jaxpr/reduce_sum | solution.py:103
  155.0 6.8 %reduce_sum.76 = f32[8,32,64]{0,2,1:T(8,128)S(1)} reduce(f32[8,32,2,64,4]{0,4,3,2,1:T(4,128)} %bitcast.192, f32[]{:T(128)} %constant.379.clone.1..sunk), dimensions={2,4}, to_apply=%region_7.7 | reduce | flops 114688 | bytes 589828 | tf_op jit(solution)/shard_map/while/body/eval_jaxpr/reduce_sum | solution.py:103
  161.8 7.8 %reduce_sum.74 = f32[8,32,64]{0,2,1:T(8,128)} reduce(f32[8,32,2,64,4]{0,4,3,2,1:T(4,128)} %bitcast.191, f32[]{:T(128)} %constant.379.clone.1..sunk), dimensions={2,4}, to_apply=%region_9.9 | reduce | flops 114688 | bytes 589828 | tf_op jit(solution)/shard_map/while/body/eval_jaxpr/reduce_sum | solution.py:103
  169.6 7.9 %reduce_sum.75 = f32[8,32,64]{0,2,1:T(8,128)} reduce(f32[8,32,2,64,4]{0,4,3,2,1:T(4,128)} %bitcast.190, f32[]{:T(128)} %constant.379.clone.1..sunk), dimensions={2,4}, to_apply=%region_8.8 | reduce | flops 114688 | bytes 589828 | tf_op jit(solution)/shard_map/while/body/eval_jaxpr/reduce_sum | solution.py:103
  177.5 3.1 bitcast_divide_fusion.2
  180.6 1.6 copy.138
  183.2 1.6 copy.139
  187.7 4.8 %copy.133 = f32[8,1,64,256]{0,3,2,1:T(8,128)} copy(f32[8,1,64,256]{3,0,2,1:T(8,128)S(1)} %get-tuple-element.167) | data formatting | bytes 1048576 | tf_op jit(solution)/shard_map/while
  194.3 5.6 %copy.134 = f32[8,1,64,256]{0,3,2,1:T(8,128)} copy(f32[8,1,64,256]{3,0,2,1:T(8,128)} %get-tuple-element.169) | data formatting | bytes 1048576 | tf_op jit(solution)/shard_map/while
  199.9 4.8 %copy.135 = f32[8,1,64,256]{0,3,2,1:T(8,128)} copy(f32[8,1,64,256]{3,0,2,1:T(8,128)S(1)} %get-tuple-element.170) | data formatting | bytes 1048576 | tf_op jit(solution)/shard_map/while
  204.7 4.8 %copy.136 = f32[8,1,64,256]{0,3,2,1:T(8,128)} copy(f32[8,1,64,256]{3,0,2,1:T(8,128)S(1)} %get-tuple-element.171) | data formatting | bytes 1048576 | tf_op jit(solution)/shard_map/while
  209.5 22.1 %multiply_subtract_fusion.2 = (f32[8,1,64,256]{0,3,2,1:T(8,128)}, f32[8,1,64,256]{0,3,2,1:T(8,128)}, f32[8,1,64,256]{0,3,2,1:T(8,128)}, f32[8,1,64,256]{0,3,2,1:T(8,128)}) fusion(f32[8,1,64,256]{0,3,2,1:T(8,128)} %copy.133, f32[8,1,64,256]{0,3,2,1:T(8,128)} %copy.134, f32[8,1,64,256]{0,3,2,1:T(8,128)} %copy.135, f32[8,1,64,256]{0,3,2,1:T(8,128)} %copy.136), kind=kLoop, calls=%fused_computation.14.clone.1 | loop fusion | flops 1572864 | bytes 4194304 | tf_op jit(solution)/shard_map/while/body/eval_jaxpr/sub | solution.py:152
  231.6 6.8 %reduce_sum.73 = f32[8,32,64]{0,2,1:T(8,128)S(1)} reduce(f32[8,32,2,64,4]{0,4,3,2,1:T(4,128)} %bitcast.193, f32[]{:T(128)} %constant.379.clone.1..sunk), dimensions={2,4}, to_apply=%region_6.6 | reduce | flops 114688 | bytes 589828 | tf_op jit(solution)/shard_map/while/body/eval_jaxpr/reduce_sum | solution.py:103
  238.4 6.8 %reduce_sum.76 = f32[8,32,64]{0,2,1:T(8,128)S(1)} reduce(f32[8,32,2,64,4]{0,4,3,2,1:T(4,128)} %bitcast.192, f32[]{:T(128)} %constant.379.clone.1..sunk), dimensions={2,4}, to_apply=%region_7.7 | reduce | flops 114688 | bytes 589828 | tf_op jit(solution)/shard_map/while/body/eval_jaxpr/reduce_sum | solution.py:103
  245.3 7.8 %reduce_sum.74 = f32[8,32,64]{0,2,1:T(8,128)} reduce(f32[8,32,2,64,4]{0,4,3,2,1:T(4,128)} %bitcast.191, f32[]{:T(128)} %constant.379.clone.1..sunk), dimensions={2,4}, to_apply=%region_9.9 | reduce | flops 114688 | bytes 589828 | tf_op jit(solution)/shard_map/while/body/eval_jaxpr/reduce_sum | solution.py:103
  253.1 7.9 %reduce_sum.75 = f32[8,32,64]{0,2,1:T(8,128)} reduce(f32[8,32,2,64,4]{0,4,3,2,1:T(4,128)} %bitcast.190, f32[]{:T(128)} %constant.379.clone.1..sunk), dimensions={2,4}, to_apply=%region_8.8 | reduce | flops 114688 | bytes 589828 | tf_op jit(solution)/shard_map/while/body/eval_jaxpr/reduce_sum | solution.py:103
  261.0 3.1 bitcast_divide_fusion.2
  281.7 3.7 %collective-permute-start = (f32[2,16,32,16]{3,2,1,0:T(8,128)S(1)}, f32[2,16,32,16]{3,2,1,0:T(8,128)S(1)}, u32[]{:S(2)}, u32[]{:S(2)}) collective-permute-start(f32[2,16,32,16]{3,2,1,0:T(8,128)S(1)} %get-tuple-element.105), channel_id=1, source_target_pairs={{0,1},{1,2},{2,3},{4,5},{5,6},{6,7},{8,9},{9,10},{10,11},{12,13},{... | collective-permute-start | bytes 196616 | tf_op jit(solution)/shard_map/ppermute | solution.py:22
  285.4 1.9 collective-permute-start.1
  287.3 4.1 %collective-permute-done = f32[2,16,32,16]{3,2,1,0:T(8,128)S(1)} collective-permute-done((f32[2,16,32,16]{3,2,1,0:T(8,128)S(1)}, f32[2,16,32,16]{3,2,1,0:T(8,128)S(1)}, u32[]{:S(2)}, u32[]{:S(2)}) %collective-permute-start) | collective-permute-done | bytes 65568 | tf_op jit(solution)/shard_map/ppermute | solution.py:22
  291.5 4.4 %collective-permute-done.1 = f32[2,16,32,16]{3,2,1,0:T(8,128)S(1)} collective-permute-done((f32[2,16,32,16]{3,2,1,0:T(8,128)S(1)}, f32[2,16,32,16]{3,2,1,0:T(8,128)S(1)}, u32[]{:S(2)}, u32[]{:S(2)}) %collective-permute-start.1) | collective-permute-done | bytes 65568 | tf_op jit(solution)/shard_map/ppermute | solution.py:25
  295.9 1.8 fusion.8
  (128 shorter events, 47.4 us)
Async XLA Ops:
  7.2 85.5 %all-gather.3.cloned.1.call-start = ((), (), s32[]{:S(2)}) async-start(), calls=%async_computation | async-start | bytes 5242880 | tf_op jit(solution)/shard_map/all_gather | solution.py:129
  102.9 192.9 %copy-start.7 = (s32[160]{0:T(256)S(1)}, s32[160]{0:T(256)}, u32[]{:S(2)}) copy-start(s32[160]{0:T(256)} %get-tuple-element.112) | copy-start | bytes 1924
  177.5 8.4 %copy-start.2 = (f32[2,8,32,64]{3,2,1,0:T(8,128)S(1)}, f32[2,8,32,64]{3,2,1,0:T(8,128)}, u32[]{:S(2)}) copy-start(f32[2,8,32,64]{3,2,1,0:T(8,128)} %get-tuple-element.187) | copy-start | bytes 393220 | tf_op jit(solution)/shard_map/while
  186.0 0.7 copy-start.3
  261.0 8.4 %copy-start.2 = (f32[2,8,32,64]{3,2,1,0:T(8,128)S(1)}, f32[2,8,32,64]{3,2,1,0:T(8,128)}, u32[]{:S(2)}) copy-start(f32[2,8,32,64]{3,2,1,0:T(8,128)} %get-tuple-element.187) | copy-start | bytes 393220 | tf_op jit(solution)/shard_map/while
  269.4 0.7 copy-start.3
  280.1 20.1 %copy-start = (f32[160,160]{1,0:T(8,128)S(1)}, f32[160,160]{1,0:T(8,128)}, u32[]{:S(2)}) copy-start(f32[160,160]{1,0:T(8,128)} %gather_fusion.7) | copy-start | bytes 307204
  280.1 20.1 %copy-start.5 = (s32[160]{0:T(256)S(1)}, s32[160]{0:T(256)}, u32[]{:S(2)}) copy-start(s32[160]{0:T(256)} %get-tuple-element.111) | copy-start | bytes 1924
  280.2 20.8 %copy-start.1 = (f32[160,160]{1,0:T(8,128)S(1)}, f32[160,160]{1,0:T(8,128)}, u32[]{:S(2)}) copy-start(f32[160,160]{1,0:T(8,128)} %gather_fusion.9) | copy-start | bytes 307204
  280.2 23.3 %copy-start.4 = (f32[160,160]{1,0:T(8,128)S(1)}, f32[160,160]{1,0:T(8,128)}, u32[]{:S(2)}) copy-start(f32[160,160]{1,0:T(8,128)} %gather_fusion.11) | copy-start | bytes 307204
  281.7 9.8 %collective-permute-start = (f32[2,16,32,16]{3,2,1,0:T(8,128)S(1)}, f32[2,16,32,16]{3,2,1,0:T(8,128)S(1)}, u32[]{:S(2)}, u32[]{:S(2)}) collective-permute-start(f32[2,16,32,16]{3,2,1,0:T(8,128)S(1)} %get-tuple-element.105), channel_id=1, source_target_pairs={{0,1},{1,2},{2,3},{4,5},{5,6},{6,7},{8,9},{9,10},{10,11},{12,13},{... | collective-permute-start | bytes 196616 | tf_op jit(solution)/shard_map/ppermute | solution.py:22
  285.4 10.5 %collective-permute-start.1 = (f32[2,16,32,16]{3,2,1,0:T(8,128)S(1)}, f32[2,16,32,16]{3,2,1,0:T(8,128)S(1)}, u32[]{:S(2)}, u32[]{:S(2)}) collective-permute-start(f32[2,16,32,16]{3,2,1,0:T(8,128)S(1)} %get-tuple-element.106), channel_id=1, source_target_pairs={{1,0},{2,1},{3,2},{5,4},{6,5},{7,6},{9,8},{10,9},{11,10},{13,12},{... | collective-permute-start | bytes 196616 | tf_op jit(solution)/shard_map/ppermute | solution.py:25
  303.4 7.3 %copy-start.6 = (s32[160]{0:T(256)S(1)}, s32[160]{0:T(256)}, u32[]{:S(2)}) copy-start(s32[160]{0:T(256)} %broadcast_add_fusion.1) | copy-start | bytes 1924
Sparse Core Ops, SparseCore 0:
  9.7 82.8 all-gather.2
where the time goes:
time: 326 us; the launch traced here: 320 us
  other arithmetic  118 us (36%)
  waiting for transfers between devices  79.6 us (24%)
  local copies, waits for them, and re-layouts  75.1 us (23%)
  matrix products  15.8 us (5%)
  between operations  14.7 us (5%)
  loops' own time  10.5 us (3%)
  starting transfers between devices  5.66 us (2%)
    all_gather x1, waiting for transfers between devices, local(): piece = lax.all_gather(flat_tiles, 'date', axis=0, tiled=True)  71.1 us
    reduce_sum x8, other arithmetic, look_mean(): field.reshape(group_size, PATCH, AZ, local_cols, RG).mean(axis=(2, 4))  58.7 us
    sub x2, other arithmetic, look_block(): imag_prod = first[:, 1] * second[:, 0] - first[:, 0] * second[:, 1]  44.2 us
    while x16, local copies, waits for them, and re-layouts  41.5 us
    another operation x1, loops' own time, local(): looked_real, looked_imag, coherent = lax.map(look_block, slot_blocks)  10.5 us
    dynamic_update_slice x10, local copies, waits for them, and re-layouts, local(): looked_real, looked_imag, coherent = lax.map(look_block, slot_blocks)  8.34 us
    dot_general x12, matrix products, cols_apply(): return jnp.matmul(field, table, precision=HIGHEST)  7.32 us
    dot_general x9, matrix products, rows_apply(): return jnp.einsum('kr,prx->pkx', table, field, precision=HIGHEST)  6.65 us
  transfers between devices with their start and end apart: 3, of which 3 were waited for; matrix products, arithmetic and copies ran while one was open for 4% of the time, Pallas kernels for 0%

commit v1 on v0

v1 whole, which is shorter than its diff:
```python
import functools
import math

import jax
import jax.numpy as jnp
import ml_dtypes
import numpy as np
from jax import lax
from jax.experimental import pallas as pl
from jax.experimental.pallas import tpu as pltpu
from jax.sharding import PartitionSpec as P

REQ = 2
AZ = 2
RG = 4
PATCH = 32
HALF = PATCH // 2
GROUP = 4
LANES = 128
MESH = pl.DeviceIdType.MESH
F32 = jnp.float32
BF16 = jnp.bfloat16


def split(value):
    high = value.astype(BF16)
    low = (value - high.astype(F32)).astype(BF16)
    return high, low


def dot(a, b):
    return jnp.dot(a, b, preferred_element_type=F32)


def dot_nt(a, b):
    return lax.dot_general(a, b, (((1,), (1,)), ((), ())), preferred_element_type=F32)


def np_split(table):
    high = table.astype(np.float32).astype(ml_dtypes.bfloat16)
    low = (table - high.astype(np.float64)).astype(np.float32).astype(ml_dtypes.bfloat16)
    return high, low


def look_table(cols):
    looked = cols // RG
    hit = np.arange(cols)[None, :] // RG == np.arange(looked)[:, None]
    return (hit / (AZ * RG)).astype(np.float32).astype(ml_dtypes.bfloat16)


def blocks(small):
    size = small.shape[0] * small.shape[1]
    small = small.reshape(size, size)
    return np.kron(np.eye(GROUP), small)


def filter_tables(looked):
    count = looked // HALF + 1
    index = np.arange(PATCH)
    angle = 2.0 * math.pi / PATCH * ((index[:, None] * index[None, :]) % PATCH)
    cos, sin = np.cos(angle), np.sin(angle)
    wide = looked + PATCH
    fwd_cos = np.zeros((count * PATCH, wide))
    fwd_sin = np.zeros((count * PATCH, wide))
    inv_cos = np.zeros((looked, count * PATCH))
    inv_sin = np.zeros((looked, count * PATCH))
    weight = np.sin(math.pi * (index + 0.5) / PATCH) ** 2 / (PATCH * PATCH)
    for k in range(count):
        rows = slice(k * PATCH, (k + 1) * PATCH)
        fwd_cos[rows, k * HALF : k * HALF + PATCH] = cos
        fwd_sin[rows, k * HALF : k * HALF + PATCH] = sin
        for u in range(PATCH):
            t = u - HALF + k * HALF
            if 0 <= t < looked:
                inv_cos[t, rows] = weight[u] * cos[u]
                inv_sin[t, rows] = weight[u] * sin[u]
    fwd_col = np.concatenate([fwd_cos, fwd_sin], axis=0)
    inv_col = np.concatenate([inv_cos, inv_sin], axis=1)

    def pair_block(rr, ri, ir, ii):
        small = np.zeros((2, PATCH, 2, PATCH))
        small[0, :, 0], small[0, :, 1], small[1, :, 0], small[1, :, 1] = rr, ri, ir, ii
        return blocks(small)

    fwd_row = np.concatenate(
        [pair_block(cos, -sin, sin, cos), pair_block(-sin, -cos, cos, -sin)], axis=0
    )
    inv_row = np.concatenate(
        [pair_block(cos, sin, -sin, cos), pair_block(-sin, cos, -cos, -sin)], axis=1
    )
    apart = (index[:, None] - index[None, :]) % PATCH
    box = ((apart == 0) | (apart == 1) | (apart == PATCH - 1)).astype(np.float64)
    ones = np.ones((PATCH, PATCH))
    zero = np.zeros((PATCH, PATCH))
    box_row = pair_block(box, box, box, box).astype(np.float32).astype(ml_dtypes.bfloat16)
    sum_row = pair_block(ones, zero, zero, ones).astype(np.float32).astype(ml_dtypes.bfloat16)
    return (
        *np_split(fwd_col),
        *np_split(fwd_row),
        box_row,
        sum_row,
        *np_split(inv_row),
        *np_split(inv_col),
    )


def gather_kernel(
    owners, tiles, pair_count,
    pairs_ref, slc_ref, look_ref, look_t_ref, wide_ref, coh_ref,
    send, recv, low_tab, prods, powers, natural, power_looked, looked, halo_low, halo_high,
    send_sem, recv_sem, halo_send_sem, halo_recv_sem,
):
    me = lax.axis_index("date")
    tile = lax.axis_index("tile")
    dates_here = slc_ref.shape[0]
    half_rows = slc_ref.shape[2] // AZ
    cols = slc_ref.shape[3]
    local_cols = cols // RG

    barrier = pltpu.get_barrier_semaphore()
    for offset in range(1, owners):
        pl.semaphore_signal(
            barrier, inc=1, device_id={"date": lax.rem(me + offset, owners)}, device_id_type=MESH
        )

    @pl.when(tile > 0)
    def _():
        pl.semaphore_signal(barrier, inc=1, device_id={"tile": tile - 1}, device_id_type=MESH)

    @pl.when(tile < tiles - 1)
    def _():
        pl.semaphore_signal(barrier, inc=1, device_id={"tile": tile + 1}, device_id_type=MESH)

    def ends(block, source):
        first = source * dates_here

        def step(i, carry):
            low, high = carry
            for c in range(2):
                date = pairs_ref[block * pair_count + i, c] - first
                inside = (date >= 0) & (date < dates_here)
                low = jnp.where(inside, jnp.minimum(low, date), low)
                high = jnp.where(inside, jnp.maximum(high, date), high)
            return low, high

        low, high = lax.fori_loop(
            0, pair_count, step, (jnp.int32(dates_here - 1), jnp.int32(0)), unroll=True
        )
        return low, high

    def stage(target, low, high):
        for rank, pick in ((0, low), (1, high)):
            for part in range(2):
                for lane in range(cols // LANES):
                    target[rank, part, lane] = slc_ref[
                        pick, part, :, lane * LANES : (lane + 1) * LANES
                    ]

    def date_copy(offset, source, target):
        return pltpu.make_async_remote_copy(
            src_ref=send.at[offset - 1],
            dst_ref=recv.at[source],
            send_sem=send_sem.at[offset - 1],
            recv_sem=recv_sem.at[source],
            device_id={"date": target},
            device_id_type=MESH,
        )

    for offset in range(1, owners):
        target = lax.rem(me + offset, owners)
        low, high = ends(target, me)
        stage(send.at[offset - 1], low, high)
        if offset == 1:
            below = lax.div(tile + tiles - 1, tiles)
            above = lax.div(2 * (tiles - 1) - tile, tiles)
            pl.semaphore_wait(barrier, owners - 1 + below + above)

        date_copy(offset, me, target).start()

    low, high = ends(me, me)
    stage(recv.at[me], low, high)
    for source in range(owners):
        low, _ = ends(me, jnp.int32(source))
        low_tab[source] = low + source * dates_here

    for offset in range(1, owners):
        source = lax.rem(me + owners - offset, owners)
        date_copy(offset, source, source).wait_recv()

    def slot(i, c):
        date = pairs_ref[me * pair_count + i, c]
        source = lax.div(date, jnp.int32(dates_here))
        rank = jnp.where(date == low_tab[source], 0, 1)
        return source, rank

    def product(i, _):
        sa, ra = slot(i, 0)
        sb, rb = slot(i, 1)
        for lane in range(cols // LANES):
            real = jnp.zeros((half_rows, LANES), F32)
            imag = jnp.zeros((half_rows, LANES), F32)
            for odd in range(AZ):
                rows = pl.ds(odd, half_rows, stride=AZ)
                a0, a1 = recv[sa, ra, 0, lane, rows, :], recv[sa, ra, 1, lane, rows, :]
                b0, b1 = recv[sb, rb, 0, lane, rows, :], recv[sb, rb, 1, lane, rows, :]
                real = real + (a0 * b0 + a1 * b1)
                imag = imag + (a1 * b0 - a0 * b1)
            prods[i, 0, :, lane * LANES : (lane + 1) * LANES] = real
            prods[i, 1, :, lane * LANES : (lane + 1) * LANES] = imag
        return 0

    lax.fori_loop(0, pair_count, product, 0)
    high, low = split(prods[...].reshape(pair_count * 2 * half_rows, cols))
    table = look_ref[...]
    looked[...] = dot_nt(table, high) + dot_nt(table, low)

    def halo_copy(up):
        step = 1 if up else -1
        return pltpu.make_async_remote_copy(
            src_ref=looked.at[pl.ds(local_cols - HALF if up else 0, HALF)],
            dst_ref=halo_low if up else halo_high,
            send_sem=halo_send_sem.at[0 if up else 1],
            recv_sem=halo_recv_sem.at[0 if up else 1],
            device_id={"tile": tile + step},
            device_id_type=MESH,
        )

    @pl.when(tile < tiles - 1)
    def _():
        halo_copy(True).start()

    @pl.when(tile > 0)
    def _():
        halo_copy(False).start()

    table_t = look_t_ref[...]
    natural[...] = (dot(high, table_t) + dot(low, table_t)).reshape(natural.shape)

    def power(i, _):
        for rank in range(REQ):
            for lane in range(cols // LANES):
                total = jnp.zeros((half_rows, LANES), F32)
                for part in range(2):
                    for odd in range(AZ):
                        field = recv[i, rank, part, lane, pl.ds(odd, half_rows, stride=AZ), :]
                        total = total + field * field
                powers[i, rank, :, lane * LANES : (lane + 1) * LANES] = total
        return 0

    lax.fori_loop(0, owners, power, 0)
    high, low = split(powers[...].reshape(owners * REQ * half_rows, cols))
    power_looked[...] = (dot(high, table_t) + dot(low, table_t)).reshape(power_looked.shape)

    def coherence(i, _):
        sa, ra = slot(i, 0)
        sb, rb = slot(i, 1)
        real, imag = natural[i, 0], natural[i, 1]
        coh_ref[i] = (real * real + imag * imag) / (power_looked[sa, ra] * power_looked[sb, rb])
        return 0

    lax.fori_loop(0, pair_count, coherence, 0)
    wide_ref[pl.ds(HALF, local_cols)] = looked[...]

    @pl.when(tile > 0)
    def _():
        halo_copy(True).wait_recv()
        wide_ref[pl.ds(0, HALF)] = halo_low[...]

    @pl.when(tile == 0)
    def _():
        wide_ref[pl.ds(0, HALF)] = jnp.zeros(halo_low.shape, F32)

    @pl.when(tile < tiles - 1)
    def _():
        halo_copy(False).wait_recv()
        wide_ref[pl.ds(HALF + local_cols, HALF)] = halo_high[...]

    @pl.when(tile == tiles - 1)
    def _():
        wide_ref[pl.ds(HALF + local_cols, HALF)] = jnp.zeros(halo_high.shape, F32)

    @pl.when(tile < tiles - 1)
    def _():
        halo_copy(True).wait_send()

    @pl.when(tile > 0)
    def _():
        halo_copy(False).wait_send()

    for offset in range(1, owners):
        date_copy(offset, me, lax.rem(me + offset, owners)).wait_send()


def filter_kernel(
    wide_ref, coh_in, fch, fcl, frh, frl, box_ref, sum_ref, irh, irl, ich, icl, out_ref, coh_out
):
    coh_out[...] = coh_in[...]
    lanes = wide_ref.shape[1]
    width = frh.shape[1]
    span = fch.shape[0] // 2
    count = span // PATCH
    high, low = split(wide_ref[...])
    part = dot(fch[...], high) + dot(fch[...], low) + dot(fcl[...], high)
    for g in range(lanes // width):
        at = slice(g * width, (g + 1) * width)
        both = jnp.concatenate([part[:span, at], part[span:, at]], axis=1)
        high, low = split(both)
        spec = dot(high, frh[...]) + dot(low, frh[...]) + dot(high, frl[...])
        high, low = split(spec * spec)
        rows = dot(high, box_ref[...]) + dot(low, box_ref[...])
        pieces, totals = [], []
        for k in range(count):
            r = rows[k * PATCH : (k + 1) * PATCH]
            totals.append(jnp.sum(r, axis=0, keepdims=True))
            pieces.append(r + pltpu.roll(r, 1, 0) + pltpu.roll(r, PATCH - 1, 0))
        totals += [jnp.zeros_like(totals[0])] * (-count % 8)
        high, low = split(jnp.concatenate(totals, axis=0))
        level = (dot(high, sum_ref[...]) + dot(low, sum_ref[...])) * (1.0 / (3 * PATCH * PATCH))
        inverse = 1.0 / (level + 1e-6)
        scaled = []
        for k in range(count):
            ratio = (pieces[k] * (1.0 / 9.0) + 0.1 * level[k : k + 1]) * inverse[k : k + 1]
            scaled.append(spec[k * PATCH : (k + 1) * PATCH] * lax.rsqrt(lax.rsqrt(ratio)))
        high, low = split(jnp.concatenate(scaled, axis=0))
        back = dot(high, irh[...]) + dot(low, irh[...]) + dot(high, irl[...])
        high, low = split(jnp.concatenate([back[:, :width], back[:, width:]], axis=0))
        final = dot(ich[...], high) + dot(ich[...], low) + dot(icl[...], high)
        final = final.T
        for p in range(GROUP):
            for c in range(2):
                first = (p * 2 + c) * PATCH
                out_ref[c, g * GROUP + p] = final[first : first + PATCH]


def local(slc, pairs):
    owners = lax.axis_size("date")
    tiles = lax.axis_size("tile")
    rows, cols = slc.shape[2], slc.shape[3]
    looked_cols = cols // RG
    half_rows = rows // AZ
    pair_count = pairs.shape[0] // owners
    lanes = pair_count * 2 * half_rows
    vmem = pl.BlockSpec(memory_space=pltpu.VMEM)
    smem = pl.BlockSpec(memory_space=pltpu.SMEM)
    look = look_table(cols)
    wide, coh = pl.pallas_call(
        functools.partial(gather_kernel, owners, tiles, pair_count),
        out_shape=(
            jax.ShapeDtypeStruct((looked_cols + PATCH, lanes), F32),
            jax.ShapeDtypeStruct((pair_count, half_rows, looked_cols), F32),
        ),
        in_specs=[smem, vmem, vmem, vmem],
        out_specs=(vmem, vmem),
        scratch_shapes=[
            pltpu.VMEM((owners - 1, REQ, 2, cols // LANES, rows, LANES), F32),
            pltpu.VMEM((owners, REQ, 2, cols // LANES, rows, LANES), F32),
            pltpu.SMEM((owners,), jnp.int32),
            pltpu.VMEM((pair_count, 2, half_rows, cols), F32),
            pltpu.VMEM((owners, REQ, half_rows, cols), F32),
            pltpu.VMEM((pair_count, 2, half_rows, looked_cols), F32),
            pltpu.VMEM((owners, REQ, half_rows, looked_cols), F32),
            pltpu.VMEM((looked_cols, lanes), F32),
            pltpu.VMEM((HALF, lanes), F32),
            pltpu.VMEM((HALF, lanes), F32),
            pltpu.SemaphoreType.DMA((owners - 1,)),
            pltpu.SemaphoreType.DMA((owners,)),
            pltpu.SemaphoreType.DMA((2,)),
            pltpu.SemaphoreType.DMA((2,)),
        ],
        compiler_params=pltpu.CompilerParams(
            collective_id=0, has_side_effects=True, vmem_limit_bytes=40 * 2**20
        ),
        name="gather_looks",
    )(pairs, slc, look, np.ascontiguousarray(look.T))
    tables = filter_tables(looked_cols)
    return pl.pallas_call(
        filter_kernel,
        out_shape=(
            jax.ShapeDtypeStruct((2, pair_count, half_rows, looked_cols), F32),
            jax.ShapeDtypeStruct(coh.shape, F32),
        ),
        in_specs=[vmem] * (2 + len(tables)),
        out_specs=(vmem, vmem),
        compiler_params=pltpu.CompilerParams(vmem_limit_bytes=40 * 2**20),
        name="filter_patches",
    )(wide, coh, *tables)


def solution(mesh):
    placed = (P("date", None, "groups", "tile"), P())
    return jax.shard_map(
        local,
        mesh=mesh,
        in_specs=placed,
        out_specs=(P(None, "date", "groups", "tile"), P("date", "groups", "tile")),
        check_vma=False,
    )
```

time: 326 us -> 47.8 us (0.15)
  the two profiles are of different devices: /device:TPU:1 before, /device:TPU:9 now
where the time goes in v1:
time: 47.8 us; the launch traced here: 47.3 us
  Pallas kernels  38.7 us (81%)
  local copies, waits for them, and re-layouts  7.98 us (17%)
  between operations  0.7 us (1%)
    pallas_call x1, Pallas kernels, local(): pl.pallas_call(functools.partial(gather_kernel, owners, tiles, pair_count...  32.1 us
    unnamed x27, local copies, waits for them, and re-layouts  7.98 us
    pallas_call x1, Pallas kernels, local(): pl.pallas_call(filter_kernel, out_shape=(jax.ShapeDtypeStruct((2, pair_co...  6.57 us

profile of v1, /device:TPU:9, one launch (start us, length us, event | category | flops | bytes accessed | tf_op | source)
XLA Modules:
  0.0 47.3 jit_solution(4563668436268324205)
XLA Ops:
  0.6 0.0 copy-start.12
  0.6 0.8 %copy.16.pairs_ref = s32[64,2]{1,0:T(8,128)S(1)} copy(s32[64,2]{0,1:T(2,128)} %param.15) | data formatting | bytes 1024 | tf_op args[1]
  1.4 0.0 copy-done.12
  1.4 0.0 copy-start
  1.4 1.1 %copy-done = f32[6,2,64,256]{3,2,1,0:T(8,128)S(1)} copy-done((f32[6,2,64,256]{3,2,1,0:T(8,128)S(1)}, f32[6,2,64,256]{3,2,1,0:T(8,128)}, u32[]{:S(2)}) %copy-start) | copy-done | bytes 786456
  2.6 0.0 copy-start.9
  2.6 0.8 %copy-done.9 = bf16[256,64]{1,0:T(8,128)(2,1)S(1)} copy-done((bf16[256,64]{1,0:T(8,128)(2,1)S(1)}, bf16[256,64]{1,0:T(8,128)(2,1)}, u32[]{:S(2)}) %copy-start.9) | copy-done | bytes 32792
  3.4 0.0 copy-start.1
  3.4 0.0 copy-start.2
  3.4 0.0 copy-start.3
  3.4 0.0 copy-start.5
  3.4 32.1 %gather_looks.1 = (f32[96,1024]{1,0:T(8,128)S(1)}, f32[16,32,64]{2,1,0:T(8,128)S(1)}) custom-call(s32[64,2]{1,0:T(8,128)S(1)} %copy.16.pairs_ref, f32[6,2,64,256]{3,2,1,0:T(8,128)S(1)} %copy-done, bf16[64,256]{1,0:T(8,128)(2,1)S(1)} %copy-done.12, bf16[256,64]{1,0:T(8,128)(2,1)S(1)} %copy-done.9), custom_call_target="tpu_custom_call" | custom-call | tf_op jit(solution)/shard_map/gather_looks/pallas_call | solution.py:346
  35.5 0.0 copy-done.1
  35.5 0.0 copy-done.2
  35.5 0.0 copy-done.3
  35.5 0.0 copy-done.5
  35.5 0.0 copy-start.4
  35.5 0.9 %copy-done.4 = bf16[512,256]{1,0:T(8,128)(2,1)S(1)} copy-done((bf16[512,256]{1,0:T(8,128)(2,1)S(1)}, bf16[512,256]{1,0:T(8,128)(2,1)}, u32[]{:S(2)}) %copy-start.4) | copy-done | bytes 262168
  36.5 0.0 copy-start.6
  36.5 0.9 %copy-done.6 = bf16[256,256]{1,0:T(8,128)(2,1)S(1)} copy-done((bf16[256,256]{1,0:T(8,128)(2,1)S(1)}, bf16[256,256]{1,0:T(8,128)(2,1)}, u32[]{:S(2)}) %copy-start.6) | copy-done | bytes 131096
  37.4 0.0 copy-start.7
  37.4 0.9 %copy-done.7 = bf16[320,96]{1,0:T(8,128)(2,1)S(1)} copy-done((bf16[320,96]{1,0:T(8,128)(2,1)S(1)}, bf16[320,96]{1,0:T(8,128)(2,1)}, u32[]{:S(2)}) %copy-start.7) | copy-done | bytes 61464
  38.3 0.0 copy-start.8
  38.3 0.9 %copy-done.8 = bf16[320,96]{1,0:T(8,128)(2,1)S(1)} copy-done((bf16[320,96]{1,0:T(8,128)(2,1)S(1)}, bf16[320,96]{1,0:T(8,128)(2,1)}, u32[]{:S(2)}) %copy-start.8) | copy-done | bytes 61464
  39.2 0.0 copy-start.10
  39.2 0.8 %copy-done.10 = bf16[64,320]{1,0:T(8,128)(2,1)S(1)} copy-done((bf16[64,320]{1,0:T(8,128)(2,1)S(1)}, bf16[64,320]{1,0:T(8,128)(2,1)}, u32[]{:S(2)}) %copy-start.10) | copy-done | bytes 40984
  40.0 0.0 copy-start.11
  40.0 0.8 %copy-done.11 = bf16[64,320]{1,0:T(8,128)(2,1)S(1)} copy-done((bf16[64,320]{1,0:T(8,128)(2,1)S(1)}, bf16[64,320]{1,0:T(8,128)(2,1)}, u32[]{:S(2)}) %copy-start.11) | copy-done | bytes 40984
  40.8 6.6 %filter_patches.1 = (f32[2,16,32,64]{3,2,1,0:T(8,128)}, f32[16,32,64]{2,1,0:T(8,128)}) custom-call(f32[96,1024]{1,0:T(8,128)S(1)} %get-tuple-element.4.wide_ref, f32[16,32,64]{2,1,0:T(8,128)S(1)} %get-tuple-element.5.coh_in, bf16[320,96]{1,0:T(8,128)(2,1)S(1)} %copy-done.8, bf16[320,96]{1,0:T(8,128)(2,1)S(1)} %copy-done.7, bf16[512,256]{1,0:T(8,128)(2,1)S(1)} %copy-done.4, ...), custom_call_target="tpu_custom_call" | custom-call | tf_op jit(solution)/shard_map/filter_patches/pallas_call | solution.py:376
Async XLA Ops:
  0.6 0.8 %copy-start.12 = (bf16[64,256]{1,0:T(8,128)(2,1)S(1)}, bf16[64,256]{1,0:T(8,128)(2,1)}, u32[]{:S(2)}) copy-start(bf16[64,256]{1,0:T(8,128)(2,1)} %constant.24.clone.look_ref) | copy-start | bytes 98308
  1.4 1.1 %copy-start = (f32[6,2,64,256]{3,2,1,0:T(8,128)S(1)}, f32[6,2,64,256]{3,2,1,0:T(8,128)}, u32[]{:S(2)}) copy-start(f32[6,2,64,256]{3,2,1,0:T(8,128)} %slc_ref.1) | copy-start | bytes 2359300
  2.6 0.8 %copy-start.9 = (bf16[256,64]{1,0:T(8,128)(2,1)S(1)}, bf16[256,64]{1,0:T(8,128)(2,1)}, u32[]{:S(2)}) copy-start(bf16[256,64]{1,0:T(8,128)(2,1)} %constant.25.clone.look_t_ref) | copy-start | bytes 98308
  3.4 32.1 %copy-start.1 = (bf16[256,512]{1,0:T(8,128)(2,1)S(1)}, bf16[256,512]{1,0:T(8,128)(2,1)}, u32[]{:S(2)}) copy-start(bf16[256,512]{1,0:T(8,128)(2,1)} %constant.33.clone.irl) | copy-start | bytes 786436
  3.4 32.1 %copy-start.2 = (bf16[256,512]{1,0:T(8,128)(2,1)S(1)}, bf16[256,512]{1,0:T(8,128)(2,1)}, u32[]{:S(2)}) copy-start(bf16[256,512]{1,0:T(8,128)(2,1)} %constant.32.clone.irh) | copy-start | bytes 786436
  3.4 32.1 %copy-start.3 = (bf16[512,256]{1,0:T(8,128)(2,1)S(1)}, bf16[512,256]{1,0:T(8,128)(2,1)}, u32[]{:S(2)}) copy-start(bf16[512,256]{1,0:T(8,128)(2,1)} %constant.29.clone.frl) | copy-start | bytes 786436
  3.4 32.1 %copy-start.5 = (bf16[256,256]{1,0:T(8,128)(2,1)S(1)}, bf16[256,256]{1,0:T(8,128)(2,1)}, u32[]{:S(2)}) copy-start(bf16[256,256]{1,0:T(8,128)(2,1)} %constant.31.clone.sum_ref) | copy-start | bytes 393220
  35.5 1.0 %copy-start.4 = (bf16[512,256]{1,0:T(8,128)(2,1)S(1)}, bf16[512,256]{1,0:T(8,128)(2,1)}, u32[]{:S(2)}) copy-start(bf16[512,256]{1,0:T(8,128)(2,1)} %constant.28.clone.frh) | copy-start | bytes 786436
  36.5 0.9 %copy-start.6 = (bf16[256,256]{1,0:T(8,128)(2,1)S(1)}, bf16[256,256]{1,0:T(8,128)(2,1)}, u32[]{:S(2)}) copy-start(bf16[256,256]{1,0:T(8,128)(2,1)} %constant.30.clone.box_ref) | copy-start | bytes 393220
  37.4 0.9 %copy-start.7 = (bf16[320,96]{1,0:T(8,128)(2,1)S(1)}, bf16[320,96]{1,0:T(8,128)(2,1)}, u32[]{:S(2)}) copy-start(bf16[320,96]{1,0:T(8,128)(2,1)} %constant.27.clone.fcl) | copy-start | bytes 184324
  38.3 0.9 %copy-start.8 = (bf16[320,96]{1,0:T(8,128)(2,1)S(1)}, bf16[320,96]{1,0:T(8,128)(2,1)}, u32[]{:S(2)}) copy-start(bf16[320,96]{1,0:T(8,128)(2,1)} %constant.26.clone.fch) | copy-start | bytes 184324
  39.2 0.8 %copy-start.10 = (bf16[64,320]{1,0:T(8,128)(2,1)S(1)}, bf16[64,320]{1,0:T(8,128)(2,1)}, u32[]{:S(2)}) copy-start(bf16[64,320]{1,0:T(8,128)(2,1)} %constant.35.clone.icl) | copy-start | bytes 122884
  40.0 0.8 %copy-start.11 = (bf16[64,320]{1,0:T(8,128)(2,1)S(1)}, bf16[64,320]{1,0:T(8,128)(2,1)}, u32[]{:S(2)}) copy-start(bf16[64,320]{1,0:T(8,128)(2,1)} %constant.34.clone.ich) | copy-start | bytes 122884

commit v2 on v1

v2 whole, which is shorter than its diff:
```python
import functools
import math

import jax
import jax.numpy as jnp
import ml_dtypes
import numpy as np
from jax import lax
from jax.experimental import pallas as pl
from jax.experimental.pallas import tpu as pltpu
from jax.sharding import PartitionSpec as P

REQ = 2
AZ = 2
RG = 4
PATCH = 32
HALF = PATCH // 2
GROUP = 4
LANES = 128
MESH = pl.DeviceIdType.MESH
F32 = jnp.float32
BF16 = jnp.bfloat16


def split(value):
    high = value.astype(BF16)
    low = (value - high.astype(F32)).astype(BF16)
    return high, low


def dot(a, b):
    return jnp.dot(a, b, preferred_element_type=F32)


def dot_nt(a, b):
    return lax.dot_general(a, b, (((1,), (1,)), ((), ())), preferred_element_type=F32)


def np_split(table):
    high = table.astype(np.float32).astype(ml_dtypes.bfloat16)
    low = (table - high.astype(np.float64)).astype(np.float32).astype(ml_dtypes.bfloat16)
    return high, low


def np_round(table):
    return table.astype(np.float32).astype(ml_dtypes.bfloat16)


def look_tables(cols):
    looked = cols // RG
    hit = np.arange(cols)[None, :] // RG == np.arange(looked)[:, None]
    table = np_round(hit / (AZ * RG))
    return np.ascontiguousarray(table[: LANES // RG, :LANES]), np.ascontiguousarray(table.T)


def blocks(small):
    size = small.shape[0] * small.shape[1]
    small = small.reshape(size, size)
    return np.kron(np.eye(GROUP), small)


def three(table):
    high, low = np_split(table)
    return np.concatenate([high, high, low], axis=1)


def filter_tables():
    index = np.arange(PATCH)
    angle = 2.0 * math.pi / PATCH * ((index[:, None] * index[None, :]) % PATCH)
    cos, sin = np.cos(angle), np.sin(angle)
    weight = np.sin(math.pi * (index + 0.5) / PATCH) ** 2 / (PATCH * PATCH)
    fwd_col = np.concatenate([cos, sin], axis=0)
    inv_col = np.concatenate([weight[:, None] * cos, weight[:, None] * sin], axis=1)

    def pair_block(rr, ri, ir, ii):
        small = np.zeros((2, PATCH, 2, PATCH))
        small[0, :, 0], small[0, :, 1], small[1, :, 0], small[1, :, 1] = rr, ri, ir, ii
        return blocks(small)

    fwd_row = np.concatenate(
        [pair_block(cos, -sin, sin, cos), pair_block(-sin, -cos, cos, -sin)], axis=0
    )
    inv_row = np.concatenate(
        [pair_block(cos, sin, -sin, cos), pair_block(-sin, cos, -cos, -sin)], axis=1
    )
    apart = (index[:, None] - index[None, :]) % PATCH
    box = ((apart == 0) | (apart == 1) | (apart == PATCH - 1)).astype(np.float64)
    ones = np.ones((PATCH, PATCH))
    zero = np.zeros((PATCH, PATCH))
    return (
        three(fwd_col),
        *np_split(fwd_row),
        np_round(pair_block(box, box, box, box)),
        np_round(pair_block(ones, zero, zero, ones)),
        *np_split(inv_row),
        three(inv_col),
    )


def triple(value):
    high, low = split(value)
    return jnp.concatenate([high, low, high], axis=0)


def filtered(patches, tables):
    fwd_col, frh, frl, box, ones, irh, irl, inv_col = tables
    width = frh.shape[1]
    groups = patches[0].shape[1] // width
    stacked = []
    for patch in patches:
        part = dot(fwd_col[...], triple(patch))
        for g in range(groups):
            at = slice(g * width, (g + 1) * width)
            stacked.append(jnp.concatenate([part[:PATCH, at], part[PATCH:, at]], axis=1))
    high, low = split(jnp.concatenate(stacked, axis=0))
    spec = dot(high, frh[...]) + dot(low, frh[...]) + dot(high, frl[...])
    high, low = split(spec * spec)
    rows = dot(high, box[...]) + dot(low, box[...])
    count = len(stacked)
    pieces, totals = [], []
    for k in range(count):
        r = rows[k * PATCH : (k + 1) * PATCH]
        totals.append(jnp.sum(r, axis=0, keepdims=True))
        pieces.append(r + pltpu.roll(r, 1, 0) + pltpu.roll(r, PATCH - 1, 0))
    totals += [jnp.zeros_like(totals[0])] * (-count % 8)
    high, low = split(jnp.concatenate(totals, axis=0))
    level = (dot(high, ones[...]) + dot(low, ones[...])) * (1.0 / (3 * PATCH * PATCH))
    inverse = 1.0 / (level + 1e-6)
    scaled = []
    for k in range(count):
        ratio = (pieces[k] * (1.0 / 9.0) + 0.1 * level[k : k + 1]) * inverse[k : k + 1]
        scaled.append(spec[k * PATCH : (k + 1) * PATCH] * lax.rsqrt(lax.rsqrt(ratio)))
    high, low = split(jnp.concatenate(scaled, axis=0))
    back = dot(high, irh[...]) + dot(low, irh[...]) + dot(high, irl[...])
    results = []
    for n in range(len(patches)):
        own = [back[(n * groups + g) * PATCH : (n * groups + g + 1) * PATCH] for g in range(groups)]
        real = jnp.concatenate([b[:, :width] for b in own], axis=1)
        turned = jnp.concatenate([b[:, width:] for b in own], axis=1)
        results.append(dot(inv_col[...], triple(jnp.concatenate([real, turned], axis=0))))
    return results


def gather_kernel(
    owners, tiles, pair_count, table_count,
    pairs_ref, slc_hbm, look_hbm, look_t_hbm, *refs,
):
    tables_hbm, refs = refs[:table_count], refs[table_count:]
    edges_ref, acc_ref, coh_ref = refs[:3]
    tables, refs = refs[3 : 3 + table_count], refs[3 + table_count :]
    chunks = slc_hbm.shape[3] // LANES
    slc_refs, recvs, refs = refs[:chunks], refs[chunks : 2 * chunks], refs[2 * chunks :]
    (
        look_ref, look_t_ref, send, low_tab, prods, powers, natural,
        power_looked, looked, halo_low, halo_high,
        load_sem, send_sem, recv_sem, halo_send_sem, halo_recv_sem,
    ) = refs
    me = lax.axis_index("date")
    tile = lax.axis_index("tile")
    dates_here, _, rows_here, _ = slc_hbm.shape
    half_rows = rows_here // AZ
    local_cols = chunks * LANES // RG
    chunk_cols = LANES // RG

    loads = [
        pltpu.make_async_copy(
            slc_hbm.at[:, :, :, pl.ds(h * LANES, LANES)], slc_refs[h], load_sem.at[h]
        )
        for h in range(chunks)
    ]
    for source, target in zip(
        (look_hbm, look_t_hbm, *tables_hbm), (look_ref, look_t_ref, *tables)
    ):
        loads.append(pltpu.make_async_copy(source, target, load_sem.at[len(loads)]))
    for load in loads[:chunks]:
        load.start()

    barrier = pltpu.get_barrier_semaphore()
    for offset in range(1, owners):
        pl.semaphore_signal(
            barrier, inc=1, device_id={"date": lax.rem(me + offset, owners)}, device_id_type=MESH
        )

    @pl.when(tile > 0)
    def _():
        pl.semaphore_signal(barrier, inc=1, device_id={"tile": tile - 1}, device_id_type=MESH)

    @pl.when(tile < tiles - 1)
    def _():
        pl.semaphore_signal(barrier, inc=1, device_id={"tile": tile + 1}, device_id_type=MESH)

    for load in loads[chunks:]:
        load.start()

    def ends(block, source):
        first = source * dates_here

        def step(i, carry):
            low, high = carry
            for c in range(2):
                date = pairs_ref[c, block * pair_count + i] - first
                inside = (date >= 0) & (date < dates_here)
                low = jnp.where(inside, jnp.minimum(low, date), low)
                high = jnp.where(inside, jnp.maximum(high, date), high)
            return low, high

        return lax.fori_loop(
            0, pair_count, step, (jnp.int32(dates_here - 1), jnp.int32(0)), unroll=True
        )

    def stage(target, h, low, high):
        for rank, pick in ((0, low), (1, high)):
            for part in range(2):
                target[rank, part] = slc_refs[h][pick, part]

    def date_copy(h, offset, source, target):
        return pltpu.make_async_remote_copy(
            src_ref=send.at[h, offset - 1],
            dst_ref=recvs[h].at[source],
            send_sem=send_sem.at[h, offset - 1],
            recv_sem=recv_sem.at[h, source],
            device_id={"date": target},
            device_id_type=MESH,
        )

    picks = [ends(lax.rem(me + offset, owners), me) for offset in range(1, owners)]
    below = lax.div(tile + tiles - 1, tiles)
    above = lax.div(2 * (tiles - 1) - tile, tiles)
    pl.semaphore_wait(barrier, owners - 1 + below + above)
    for h in range(chunks):
        loads[h].wait()
        for offset in range(1, owners):
            stage(send.at[h, offset - 1], h, *picks[offset - 1])
            date_copy(h, offset, me, lax.rem(me + offset, owners)).start()

    low, high = ends(me, me)
    for h in range(chunks):
        stage(recvs[h].at[me], h, low, high)
    for source in range(owners):
        low, _ = ends(me, jnp.int32(source))
        low_tab[source] = low + source * dates_here
    acc_ref[...] = jnp.zeros(acc_ref.shape, F32)
    for load in loads[chunks:]:
        load.wait()

    def slot(i, c):
        date = pairs_ref[c, me * pair_count + i]
        source = lax.div(date, jnp.int32(dates_here))
        rank = jnp.where(date == low_tab[source], 0, 1)
        return source, rank

    def halo_copy(up):
        step = 1 if up else -1
        return pltpu.make_async_remote_copy(
            src_ref=looked.at[pl.ds(local_cols - HALF if up else 0, HALF)],
            dst_ref=halo_low if up else halo_high,
            send_sem=halo_send_sem.at[0 if up else 1],
            recv_sem=halo_recv_sem.at[0 if up else 1],
            device_id={"tile": tile + step},
            device_id_type=MESH,
        )

    for h in range(chunks):
        for offset in range(1, owners):
            source = lax.rem(me + owners - offset, owners)
            date_copy(h, offset, source, source).wait_recv()

        recv = recvs[h]

        def product(i, _):
            sa, ra = slot(i, 0)
            sb, rb = slot(i, 1)
            real = jnp.zeros((half_rows, LANES), F32)
            imag = jnp.zeros((half_rows, LANES), F32)
            for odd in range(AZ):
                rows = pl.ds(odd, half_rows, stride=AZ)
                a0, a1 = recv[sa, ra, 0, rows, :], recv[sa, ra, 1, rows, :]
                b0, b1 = recv[sb, rb, 0, rows, :], recv[sb, rb, 1, rows, :]
                real = real + (a0 * b0 + a1 * b1)
                imag = imag + (a1 * b0 - a0 * b1)
            prods[i, 0] = real
            prods[i, 1] = imag
            return 0

        lax.fori_loop(0, pair_count, product, 0)
        high, low = split(prods[...].reshape(pair_count * 2 * half_rows, LANES))
        table = look_ref[...]
        looked[pl.ds(h * chunk_cols, chunk_cols)] = dot_nt(table, high) + dot_nt(table, low)

        if h == 0:

            @pl.when(tile > 0)
            def _():
                halo_copy(False).start()

        if h == chunks - 1:

            @pl.when(tile < tiles - 1)
            def _():
                halo_copy(True).start()

        table = look_t_ref[pl.ds(h * LANES, LANES)]
        new = (dot(high, table) + dot(low, table)).reshape(natural.shape)
        natural[...] = new if h == 0 else natural[...] + new

        def power(i, _):
            for rank in range(REQ):
                total = jnp.zeros((half_rows, LANES), F32)
                for part in range(2):
                    for odd in range(AZ):
                        field = recv[i, rank, part, pl.ds(odd, half_rows, stride=AZ), :]
                        total = total + field * field
                powers[i, rank] = total
            return 0

        lax.fori_loop(0, owners, power, 0)
        high, low = split(powers[...].reshape(owners * REQ * half_rows, LANES))
        new = (dot(high, table) + dot(low, table)).reshape(power_looked.shape)
        power_looked[...] = new if h == 0 else power_looked[...] + new

        per_chunk = chunk_cols // HALF
        inner = [k for k in range(h * per_chunk, (h + 1) * per_chunk) if k > 0]
        results = filtered([looked[pl.ds((k - 1) * HALF, PATCH)] for k in inner], tables)
        for k, result in zip(inner, results):
            acc_ref[pl.ds((k - 1) * HALF, PATCH)] += result

    def coherence(i, _):
        sa, ra = slot(i, 0)
        sb, rb = slot(i, 1)
        real, imag = natural[i, 0], natural[i, 1]
        coh_ref[i] = (real * real + imag * imag) / (power_looked[sa, ra] * power_looked[sb, rb])
        return 0

    lax.fori_loop(0, pair_count, coherence, 0)
    edges_ref[0, pl.ds(HALF, HALF)] = looked[pl.ds(0, HALF)]
    edges_ref[1, pl.ds(0, HALF)] = looked[pl.ds(local_cols - HALF, HALF)]

    @pl.when(tile > 0)
    def _():
        halo_copy(True).wait_recv()
        edges_ref[0, pl.ds(0, HALF)] = halo_low[...]

    @pl.when(tile == 0)
    def _():
        edges_ref[0, pl.ds(0, HALF)] = jnp.zeros(halo_low.shape, F32)

    @pl.when(tile < tiles - 1)
    def _():
        halo_copy(False).wait_recv()
        edges_ref[1, pl.ds(HALF, HALF)] = halo_high[...]

    @pl.when(tile == tiles - 1)
    def _():
        edges_ref[1, pl.ds(HALF, HALF)] = jnp.zeros(halo_high.shape, F32)

    @pl.when(tile < tiles - 1)
    def _():
        halo_copy(True).wait_send()

    @pl.when(tile > 0)
    def _():
        halo_copy(False).wait_send()

    for h in range(chunks):
        for offset in range(1, owners):
            date_copy(h, offset, me, lax.rem(me + offset, owners)).wait_send()


def filter_kernel(edges_ref, acc_ref, coh_in, *refs):
    tables, (out_ref, coh_out) = refs[:-2], refs[-2:]
    coh_out[...] = coh_in[...]
    first, last = filtered([edges_ref[0], edges_ref[1]], tables)
    final = jnp.concatenate(
        [
            acc_ref[:HALF] + first[HALF:],
            acc_ref[HALF:-HALF],
            acc_ref[-HALF:] + last[:HALF],
        ],
        axis=0,
    ).T
    for p in range(out_ref.shape[1]):
        for c in range(2):
            at = (p * 2 + c) * PATCH
            out_ref[c, p] = final[at : at + PATCH]


def local(slc, pairs):
    owners = lax.axis_size("date")
    tiles = lax.axis_size("tile")
    rows, cols = slc.shape[2], slc.shape[3]
    looked_cols = cols // RG
    half_rows = rows // AZ
    chunks = cols // LANES
    pair_count = pairs.shape[0] // owners
    lanes = pair_count * 2 * half_rows
    vmem = pl.BlockSpec(memory_space=pltpu.VMEM)
    smem = pl.BlockSpec(memory_space=pltpu.SMEM)
    hbm = pl.BlockSpec(memory_space=pl.ANY)
    look, look_t = look_tables(cols)
    tables = filter_tables()
    held = [jax.ShapeDtypeStruct(t.shape, t.dtype) for t in tables]
    outs = pl.pallas_call(
        functools.partial(gather_kernel, owners, tiles, pair_count, len(tables)),
        out_shape=(
            jax.ShapeDtypeStruct((2, PATCH, lanes), F32),
            jax.ShapeDtypeStruct((looked_cols, lanes), F32),
            jax.ShapeDtypeStruct((pair_count, half_rows, looked_cols), F32),
            *held,
        ),
        in_specs=[smem] + [hbm] * (3 + len(tables)),
        out_specs=(vmem,) * (3 + len(tables)),
        scratch_shapes=[
            *[pltpu.VMEM((*slc.shape[:3], LANES), F32)] * chunks,
            *[pltpu.VMEM((owners, REQ, 2, rows, LANES), F32)] * chunks,
            pltpu.VMEM(look.shape, BF16),
            pltpu.VMEM(look_t.shape, BF16),
            pltpu.VMEM((chunks, owners - 1, REQ, 2, rows, LANES), F32),
            pltpu.SMEM((owners,), jnp.int32),
            pltpu.VMEM((pair_count, 2, half_rows, LANES), F32),
            pltpu.VMEM((owners, REQ, half_rows, LANES), F32),
            pltpu.VMEM((pair_count, 2, half_rows, looked_cols), F32),
            pltpu.VMEM((owners, REQ, half_rows, looked_cols), F32),
            pltpu.VMEM((looked_cols, lanes), F32),
            pltpu.VMEM((HALF, lanes), F32),
            pltpu.VMEM((HALF, lanes), F32),
            pltpu.SemaphoreType.DMA((chunks + 2 + len(tables),)),
            pltpu.SemaphoreType.DMA((chunks, owners - 1)),
            pltpu.SemaphoreType.DMA((chunks, owners)),
            pltpu.SemaphoreType.DMA((2,)),
            pltpu.SemaphoreType.DMA((2,)),
        ],
        compiler_params=pltpu.CompilerParams(
            collective_id=0, has_side_effects=True, vmem_limit_bytes=40 * 2**20
        ),
        name="gather_looks",
    )(pairs.T, slc, look, look_t, *tables)
    return pl.pallas_call(
        filter_kernel,
        out_shape=(
            jax.ShapeDtypeStruct((2, pair_count, half_rows, looked_cols), F32),
            jax.ShapeDtypeStruct((pair_count, half_rows, looked_cols), F32),
        ),
        in_specs=[vmem] * len(outs),
        out_specs=(vmem, vmem),
        compiler_params=pltpu.CompilerParams(vmem_limit_bytes=40 * 2**20),
        name="filter_edges",
    )(*outs)


def solution(mesh):
    placed = (P("date", None, "groups", "tile"), P())
    return jax.shard_map(
        local,
        mesh=mesh,
        in_specs=placed,
        out_specs=(P(None, "date", "groups", "tile"), P("date", "groups", "tile")),
        check_vma=False,
    )
```

time: 47.8 us -> 45.1 us (0.944)
  the two profiles are of different devices: /device:TPU:9 before, /device:TPU:0 now
where the time goes in v2:
time: 45.1 us; the launch traced here: 44.6 us
  Pallas kernels  34.3 us (76%)
  local copies, waits for them, and re-layouts  9.7 us (22%)
  between operations  0.66 us (1%)
    pallas_call x1, Pallas kernels, local(): pl.pallas_call(functools.partial(gather_kernel, owners, tiles, pair_count...  31.5 us
    unnamed x24, local copies, waits for them, and re-layouts  9.7 us
    pallas_call x1, Pallas kernels, local(): pl.pallas_call(filter_kernel, out_shape=(jax.ShapeDtypeStruct((2, pair_co...  2.79 us

profile of v2, /device:TPU:0, one launch (start us, length us, event | category | flops | bytes accessed | tf_op | source)
XLA Modules:
  0.0 44.6 jit_solution(6796880042207074011)
XLA Ops:
  0.6 0.0 copy-start.8
  0.6 0.0 copy-start.11
  0.7 0.7 %copy-done.8 = bf16[32,192]{1,0:T(8,128)(2,1)S(1)} copy-done((bf16[32,192]{1,0:T(8,128)(2,1)S(1)}, bf16[32,192]{1,0:T(8,128)(2,1)}, u32[]{:S(2)}) %copy-start.8) | copy-done | bytes 12312
  1.4 0.0 copy-done.11
  1.4 0.0 copy-start
  1.4 1.1 %copy-done = f32[6,2,64,256]{3,2,1,0:T(8,128)S(1)} copy-done((f32[6,2,64,256]{3,2,1,0:T(8,128)S(1)}, f32[6,2,64,256]{3,2,1,0:T(8,128)}, u32[]{:S(2)}) %copy-start) | copy-done | bytes 786456
  2.5 0.0 copy-start.1
  2.5 0.9 %copy-done.1 = bf16[256,512]{1,0:T(8,128)(2,1)S(1)} copy-done((bf16[256,512]{1,0:T(8,128)(2,1)S(1)}, bf16[256,512]{1,0:T(8,128)(2,1)}, u32[]{:S(2)}) %copy-start.1) | copy-done | bytes 262168
  3.4 0.0 copy-start.2
  3.4 0.9 %copy-done.2 = bf16[256,512]{1,0:T(8,128)(2,1)S(1)} copy-done((bf16[256,512]{1,0:T(8,128)(2,1)S(1)}, bf16[256,512]{1,0:T(8,128)(2,1)}, u32[]{:S(2)}) %copy-start.2) | copy-done | bytes 262168
  4.4 0.0 copy-start.3
  4.4 0.9 %copy-done.3 = bf16[512,256]{1,0:T(8,128)(2,1)S(1)} copy-done((bf16[512,256]{1,0:T(8,128)(2,1)S(1)}, bf16[512,256]{1,0:T(8,128)(2,1)}, u32[]{:S(2)}) %copy-start.3) | copy-done | bytes 262168
  5.3 0.0 copy-start.4
  5.3 0.9 %copy-done.4 = bf16[512,256]{1,0:T(8,128)(2,1)S(1)} copy-done((bf16[512,256]{1,0:T(8,128)(2,1)S(1)}, bf16[512,256]{1,0:T(8,128)(2,1)}, u32[]{:S(2)}) %copy-start.4) | copy-done | bytes 262168
  6.3 0.0 copy-start.5
  6.3 0.9 %copy-done.5 = bf16[256,256]{1,0:T(8,128)(2,1)S(1)} copy-done((bf16[256,256]{1,0:T(8,128)(2,1)S(1)}, bf16[256,256]{1,0:T(8,128)(2,1)}, u32[]{:S(2)}) %copy-start.5) | copy-done | bytes 131096
  7.2 0.0 copy-start.6
  7.2 0.9 %copy-done.6 = bf16[256,256]{1,0:T(8,128)(2,1)S(1)} copy-done((bf16[256,256]{1,0:T(8,128)(2,1)S(1)}, bf16[256,256]{1,0:T(8,128)(2,1)}, u32[]{:S(2)}) %copy-start.6) | copy-done | bytes 131096
  8.1 0.0 copy-start.7
  8.1 0.8 %copy-done.7 = bf16[256,64]{1,0:T(8,128)(2,1)S(1)} copy-done((bf16[256,64]{1,0:T(8,128)(2,1)S(1)}, bf16[256,64]{1,0:T(8,128)(2,1)}, u32[]{:S(2)}) %copy-start.7) | copy-done | bytes 32792
  8.9 0.0 copy-start.9
  8.9 0.7 %copy-done.9 = bf16[64,96]{1,0:T(8,128)(2,1)S(1)} copy-done((bf16[64,96]{1,0:T(8,128)(2,1)S(1)}, bf16[64,96]{1,0:T(8,128)(2,1)}, u32[]{:S(2)}) %copy-start.9) | copy-done | bytes 12312
  9.7 0.0 copy-start.10
  9.7 0.7 %copy-done.10 = bf16[32,128]{1,0:T(8,128)(2,1)S(1)} copy-done((bf16[32,128]{1,0:T(8,128)(2,1)S(1)}, bf16[32,128]{1,0:T(8,128)(2,1)}, u32[]{:S(2)}) %copy-start.10) | copy-done | bytes 8216
  10.4 31.5 %gather_looks.1 = (f32[2,32,1024]{2,1,0:T(8,128)S(1)}, f32[64,1024]{1,0:T(8,128)S(1)}, f32[16,32,64]{2,1,0:T(8,128)S(1)}, bf16[64,96]{1,0:T(8,128)(2,1)S(1)}, bf...) custom-call(s32[2,64]{1,0:T(2,128)S(1)} %bitcast.1, ...), custom_call_target="tpu_custom_call" | custom-call | tf_op jit(solution)/shard_map/gather_looks/pallas_call | solution.py:402
  41.8 2.8 %filter_edges.1 = (f32[2,16,32,64]{3,2,1,0:T(8,128)}, f32[16,32,64]{2,1,0:T(8,128)}) custom-call(f32[2,32,1024]{2,1,0:T(8,128)S(1)} %get-tuple-element.13.edges_ref, f32[64,1024]{1,0:T(8,128)S(1)} %get-tuple-element.14.acc_ref, f32[16,32,64]{2,1,0:T(8,128)S(1)} %get-tuple-element.15.coh_in, bf16[64,96]{1,0:T(8,128)(2,1)S(1)} %get-tuple-element.16.refs_0_, ...), custom_call_target="tpu_custom_call" | custom-call | tf_op jit(solution)/shard_map/filter_edges/pallas_call | solution.py:437
Async XLA Ops:
  0.6 0.7 %copy-start.8 = (bf16[32,192]{1,0:T(8,128)(2,1)S(1)}, bf16[32,192]{1,0:T(8,128)(2,1)}, u32[]{:S(2)}) copy-start(bf16[32,192]{1,0:T(8,128)(2,1)} %constant.29.clone.refs_7_) | copy-start | bytes 36868
  0.6 0.7 %copy-start.11 = (s32[64,2]{0,1:T(2,128)S(1)}, s32[64,2]{0,1:T(2,128)}, u32[]{:S(2)}) copy-start(s32[64,2]{0,1:T(2,128)} %param.13) | copy-start | bytes 1540
  1.4 1.1 %copy-start = (f32[6,2,64,256]{3,2,1,0:T(8,128)S(1)}, f32[6,2,64,256]{3,2,1,0:T(8,128)}, u32[]{:S(2)}) copy-start(f32[6,2,64,256]{3,2,1,0:T(8,128)} %slc_hbm.1) | copy-start | bytes 2359300
  2.5 0.9 %copy-start.1 = (bf16[256,512]{1,0:T(8,128)(2,1)S(1)}, bf16[256,512]{1,0:T(8,128)(2,1)}, u32[]{:S(2)}) copy-start(bf16[256,512]{1,0:T(8,128)(2,1)} %constant.28.clone.refs_6_) | copy-start | bytes 786436
  3.4 0.9 %copy-start.2 = (bf16[256,512]{1,0:T(8,128)(2,1)S(1)}, bf16[256,512]{1,0:T(8,128)(2,1)}, u32[]{:S(2)}) copy-start(bf16[256,512]{1,0:T(8,128)(2,1)} %constant.27.clone.refs_5_) | copy-start | bytes 786436
  4.4 0.9 %copy-start.3 = (bf16[512,256]{1,0:T(8,128)(2,1)S(1)}, bf16[512,256]{1,0:T(8,128)(2,1)}, u32[]{:S(2)}) copy-start(bf16[512,256]{1,0:T(8,128)(2,1)} %constant.24.clone.refs_2_) | copy-start | bytes 786436
  5.3 0.9 %copy-start.4 = (bf16[512,256]{1,0:T(8,128)(2,1)S(1)}, bf16[512,256]{1,0:T(8,128)(2,1)}, u32[]{:S(2)}) copy-start(bf16[512,256]{1,0:T(8,128)(2,1)} %constant.23.clone.refs_1_) | copy-start | bytes 786436
  6.3 0.9 %copy-start.5 = (bf16[256,256]{1,0:T(8,128)(2,1)S(1)}, bf16[256,256]{1,0:T(8,128)(2,1)}, u32[]{:S(2)}) copy-start(bf16[256,256]{1,0:T(8,128)(2,1)} %constant.26.clone.refs_4_) | copy-start | bytes 393220
  7.2 0.9 %copy-start.6 = (bf16[256,256]{1,0:T(8,128)(2,1)S(1)}, bf16[256,256]{1,0:T(8,128)(2,1)}, u32[]{:S(2)}) copy-start(bf16[256,256]{1,0:T(8,128)(2,1)} %constant.25.clone.refs_3_) | copy-start | bytes 393220
  8.1 0.8 %copy-start.7 = (bf16[256,64]{1,0:T(8,128)(2,1)S(1)}, bf16[256,64]{1,0:T(8,128)(2,1)}, u32[]{:S(2)}) copy-start(bf16[256,64]{1,0:T(8,128)(2,1)} %constant.21.clone.look_t_hbm) | copy-start | bytes 98308
  8.9 0.7 %copy-start.9 = (bf16[64,96]{1,0:T(8,128)(2,1)S(1)}, bf16[64,96]{1,0:T(8,128)(2,1)}, u32[]{:S(2)}) copy-start(bf16[64,96]{1,0:T(8,128)(2,1)} %constant.22.clone.refs_0_) | copy-start | bytes 36868
  9.7 0.7 %copy-start.10 = (bf16[32,128]{1,0:T(8,128)(2,1)S(1)}, bf16[32,128]{1,0:T(8,128)(2,1)}, u32[]{:S(2)}) copy-start(bf16[32,128]{1,0:T(8,128)(2,1)} %constant.20.clone.look_hbm) | copy-start | bytes 24580

commit v3 on v2

--- a/solution.py
+++ b/solution.py
@@ -3,8 +3,6 @@
 
 import jax
 import jax.numpy as jnp
-import ml_dtypes
-import numpy as np
 from jax import lax
 from jax.experimental import pallas as pl
 from jax.experimental.pallas import tpu as pltpu
@@ -36,65 +34,81 @@
     return lax.dot_general(a, b, (((1,), (1,)), ((), ())), preferred_element_type=F32)
 
 
-def np_split(table):
-    high = table.astype(np.float32).astype(ml_dtypes.bfloat16)
-    low = (table - high.astype(np.float64)).astype(np.float32).astype(ml_dtypes.bfloat16)
-    return high, low
-
-
-def np_round(table):
-    return table.astype(np.float32).astype(ml_dtypes.bfloat16)
-
-
-def look_tables(cols):
-    looked = cols // RG
-    hit = np.arange(cols)[None, :] // RG == np.arange(looked)[:, None]
-    table = np_round(hit / (AZ * RG))
-    return np.ascontiguousarray(table[: LANES // RG, :LANES]), np.ascontiguousarray(table.T)
-
-
-def blocks(small):
-    size = small.shape[0] * small.shape[1]
-    small = small.reshape(size, size)
-    return np.kron(np.eye(GROUP), small)
-
-
-def three(table):
-    high, low = np_split(table)
-    return np.concatenate([high, high, low], axis=1)
-
-
-def filter_tables():
-    index = np.arange(PATCH)
-    angle = 2.0 * math.pi / PATCH * ((index[:, None] * index[None, :]) % PATCH)
-    cos, sin = np.cos(angle), np.sin(angle)
-    weight = np.sin(math.pi * (index + 0.5) / PATCH) ** 2 / (PATCH * PATCH)
-    fwd_col = np.concatenate([cos, sin], axis=0)
-    inv_col = np.concatenate([weight[:, None] * cos, weight[:, None] * sin], axis=1)
-
-    def pair_block(rr, ri, ir, ii):
-        small = np.zeros((2, PATCH, 2, PATCH))
-        small[0, :, 0], small[0, :, 1], small[1, :, 0], small[1, :, 1] = rr, ri, ir, ii
-        return blocks(small)
-
-    fwd_row = np.concatenate(
-        [pair_block(cos, -sin, sin, cos), pair_block(-sin, -cos, cos, -sin)], axis=0
+def ids(shape, axis):
+    return lax.broadcasted_iota(jnp.int32, shape, axis)
+
+
+def chosen(index, values):
+    result = jnp.zeros(index.shape, F32)
+    for i, value in enumerate(values):
+        result = jnp.where(index == i, F32(value), result)
+    return result
+
+
+def cos_turn(turn):
+    angles = [2.0 * math.pi * i / PATCH for i in range(PATCH)]
+    return chosen(turn & (PATCH - 1), [math.cos(a) for a in angles])
+
+
+def table_shapes():
+    width = GROUP * 2 * PATCH
+    return (
+        (2 * PATCH, 3 * PATCH),
+        (2 * width, width),
+        (2 * width, width),
+        (width, width),
+        (width, width),
+        (width, 2 * width),
+        (width, 2 * width),
+        (PATCH, 6 * PATCH),
     )
-    inv_row = np.concatenate(
-        [pair_block(cos, sin, -sin, cos), pair_block(-sin, cos, -cos, -sin)], axis=1
+
+
+def fill_tables(look, look_t, fwd_col, frh, frl, box, ones, irh, irl, inv_col):
+    quarter = PATCH // 4
+    pair = 2 * PATCH
+    width = GROUP * pair
+    scale = 1.0 / (AZ * RG)
+    hit = ids(look.shape, 1) // RG == ids(look.shape, 0)
+    look[...] = jnp.where(hit, F32(scale), F32(0.0)).astype(BF16)
+    hit = ids(look_t.shape, 0) // RG == ids(look_t.shape, 1)
+    look_t[...] = jnp.where(hit, F32(scale), F32(0.0)).astype(BF16)
+
+    row, col = ids(fwd_col.shape, 0), ids(fwd_col.shape, 1)
+    value = cos_turn((row & (PATCH - 1)) * (col & (PATCH - 1)) - quarter * (row >> 5))
+    high = value.astype(BF16).astype(F32)
+    fwd_col[...] = jnp.where(col < 2 * PATCH, high, value - high).astype(BF16)
+
+    row, col = ids(inv_col.shape, 0), ids(inv_col.shape, 1)
+    waves = [math.sin(math.pi * (u + 0.5) / PATCH) ** 2 / PATCH**2 for u in range(PATCH)]
+    value = chosen(row, waves) * cos_turn(
+        row * (col & (PATCH - 1)) - quarter * ((col >> 5) & 1)
     )
-    apart = (index[:, None] - index[None, :]) % PATCH
-    box = ((apart == 0) | (apart == 1) | (apart == PATCH - 1)).astype(np.float64)
-    ones = np.ones((PATCH, PATCH))
-    zero = np.zeros((PATCH, PATCH))
-    return (
-        three(fwd_col),
-        *np_split(fwd_row),
-        np_round(pair_block(box, box, box, box)),
-        np_round(pair_block(ones, zero, zero, ones)),
-        *np_split(inv_row),
-        three(inv_col),
-    )
+    high = value.astype(BF16).astype(F32)
+    inv_col[...] = jnp.where(col < 2 * pair, high, value - high).astype(BF16)
+
+    row, col = ids((pair, width), 0), ids((pair, width), 1)
+    turn = (row & (PATCH - 1)) * (col & (PATCH - 1))
+    lift = quarter * (((col >> 5) & 1) - (row >> 5))
+    apart = (row - col) & (PATCH - 1)
+    near = (apart == 0) | (apart == 1) | (apart == PATCH - 1)
+    same = (row >> 5) == ((col >> 5) & 1)
+    for block, turns in enumerate((turn + lift, turn + lift + quarter)):
+        value = cos_turn(turns)
+        for p in range(GROUP):
+            high, low = split(jnp.where(col // pair == p, value, 0.0))
+            frh[pl.ds(block * width + p * pair, pair)] = high
+            frl[pl.ds(block * width + p * pair, pair)] = low
+    for block, turns in enumerate((turn - lift, turn - lift + quarter)):
+        value = cos_turn(turns)
+        for p in range(GROUP):
+            high, low = split(jnp.where(col // pair == p, value, 0.0))
+            irh[pl.ds(p * pair, pair), pl.ds(block * width, width)] = high
+            irl[pl.ds(p * pair, pair), pl.ds(block * width, width)] = low
+    for p in range(GROUP):
+        own = col // pair == p
+        box[pl.ds(p * pair, pair)] = jnp.where(own & near, F32(1.0), F32(0.0)).astype(BF16)
+        ones[pl.ds(p * pair, pair)] = jnp.where(own & same, F32(1.0), F32(0.0)).astype(BF16)
 
 
 def triple(value):
@@ -142,10 +156,8 @@
 
 
 def gather_kernel(
-    owners, tiles, pair_count, table_count,
-    pairs_ref, slc_hbm, look_hbm, look_t_hbm, *refs,
+    owners, tiles, pair_count, table_count, pairs_ref, slc_hbm, *refs
 ):
-    tables_hbm, refs = refs[:table_count], refs[table_count:]
     edges_ref, acc_ref, coh_ref = refs[:3]
     tables, refs = refs[3 : 3 + table_count], refs[3 + table_count :]
     chunks = slc_hbm.shape[3] // LANES
@@ -168,11 +180,7 @@
         )
         for h in range(chunks)
     ]
-    for source, target in zip(
-        (look_hbm, look_t_hbm, *tables_hbm), (look_ref, look_t_ref, *tables)
-    ):
-        loads.append(pltpu.make_async_copy(source, target, load_sem.at[len(loads)]))
-    for load in loads[:chunks]:
+    for load in loads:
         load.start()
 
     barrier = pltpu.get_barrier_semaphore()
@@ -188,9 +196,6 @@
     @pl.when(tile < tiles - 1)
     def _():
         pl.semaphore_signal(barrier, inc=1, device_id={"tile": tile + 1}, device_id_type=MESH)
-
-    for load in loads[chunks:]:
-        load.start()
 
     def ends(block, source):
         first = source * dates_here
@@ -240,8 +245,7 @@
         low, _ = ends(me, jnp.int32(source))
         low_tab[source] = low + source * dates_here
     acc_ref[...] = jnp.zeros(acc_ref.shape, F32)
-    for load in loads[chunks:]:
-        load.wait()
+    fill_tables(look_ref, look_t_ref, *tables)
 
     def slot(i, c):
         date = pairs_ref[c, me * pair_count + i]
@@ -395,25 +399,23 @@
     lanes = pair_count * 2 * half_rows
     vmem = pl.BlockSpec(memory_space=pltpu.VMEM)
     smem = pl.BlockSpec(memory_space=pltpu.SMEM)
-    hbm = pl.BlockSpec(memory_space=pl.ANY)
-    look, look_t = look_tables(cols)
-    tables = filter_tables()
-    held = [jax.ShapeDtypeStruct(t.shape, t.dtype) for t in tables]
+    hbm = pl.BlockSpec(memory_space=pltpu.HBM)
+    tables = [jax.ShapeDtypeStruct(shape, BF16) for shape in table_shapes()]
     outs = pl.pallas_call(
         functools.partial(gather_kernel, owners, tiles, pair_count, len(tables)),
         out_shape=(
             jax.ShapeDtypeStruct((2, PATCH, lanes), F32),
             jax.ShapeDtypeStruct((looked_cols, lanes), F32),
             jax.ShapeDtypeStruct((pair_count, half_rows, looked_cols), F32),
-            *held,
+            *tables,
         ),
-        in_specs=[smem] + [hbm] * (3 + len(tables)),
+        in_specs=[smem, hbm],
         out_specs=(vmem,) * (3 + len(tables)),
         scratch_shapes=[
             *[pltpu.VMEM((*slc.shape[:3], LANES), F32)] * chunks,
             *[pltpu.VMEM((owners, REQ, 2, rows, LANES), F32)] * chunks,
-            pltpu.VMEM(look.shape, BF16),
-            pltpu.VMEM(look_t.shape, BF16),
+            pltpu.VMEM((LANES // RG, LANES), BF16),
+            pltpu.VMEM((cols, looked_cols), BF16),
             pltpu.VMEM((chunks, owners - 1, REQ, 2, rows, LANES), F32),
             pltpu.SMEM((owners,), jnp.int32),
             pltpu.VMEM((pair_count, 2, half_rows, LANES), F32),
@@ -423,7 +425,7 @@
             pltpu.VMEM((looked_cols, lanes), F32),
             pltpu.VMEM((HALF, lanes), F32),
             pltpu.VMEM((HALF, lanes), F32),
-            pltpu.SemaphoreType.DMA((chunks + 2 + len(tables),)),
+            pltpu.SemaphoreType.DMA((chunks,)),
             pltpu.SemaphoreType.DMA((chunks, owners - 1)),
             pltpu.SemaphoreType.DMA((chunks, owners)),
             pltpu.SemaphoreType.DMA((2,)),
@@ -433,7 +435,7 @@
             collective_id=0, has_side_effects=True, vmem_limit_bytes=40 * 2**20
         ),
         name="gather_looks",
-    )(pairs.T, slc, look, look_t, *tables)
+    )(pairs.T, slc)
     return pl.pallas_call(
         filter_kernel,
         out_shape=(

time: 45.1 us -> 36.8 us (0.82)
  local copies, waits for them, and re-layouts: 9.7 us -> 1.8 us
    unnamed x24 -> x4, local copies, waits for them, and re-layouts: 9.7 us -> 1.8 us
where the time goes in v3:
time: 36.8 us; the launch traced here: 36.6 us
  Pallas kernels  34.1 us (93%)
  local copies, waits for them, and re-layouts  1.8 us (5%)
  between operations  0.65 us (2%)
    pallas_call x1, Pallas kernels, local(): pl.pallas_call(functools.partial(gather_kernel, owners, tiles, pair_count...  31.3 us
    pallas_call x1, Pallas kernels, local(): pl.pallas_call(filter_kernel, out_shape=(jax.ShapeDtypeStruct((2, pair_co...  2.79 us
    unnamed x4, local copies, waits for them, and re-layouts  1.8 us

profile of v3, /device:TPU:0, one launch (start us, length us, event | category | flops | bytes accessed | tf_op | source)
XLA Modules:
  0.0 36.6 jit_solution(9536648911722847724)
XLA Ops:
  0.6 0.0 copy-start.1
  0.6 0.7 %copy-done.1 = s32[64,2]{0,1:T(2,128)S(1)} copy-done((s32[64,2]{0,1:T(2,128)S(1)}, s32[64,2]{0,1:T(2,128)}, u32[]{:S(2)}) %copy-start.1) | copy-done | bytes 536
  1.3 0.0 copy-start
  1.3 1.1 %copy-done = f32[6,2,64,256]{3,2,1,0:T(8,128)S(1)} copy-done((f32[6,2,64,256]{3,2,1,0:T(8,128)S(1)}, f32[6,2,64,256]{3,2,1,0:T(8,128)}, u32[]{:S(2)}) %copy-start) | copy-done | bytes 786456
  2.4 31.3 %gather_looks.1 = (f32[2,32,1024]{2,1,0:T(8,128)S(1)}, f32[64,1024]{1,0:T(8,128)S(1)}, f32[16,32,64]{2,1,0:T(8,128)S(1)}, bf16[64,96]{1,0:T(8,128)(2,1)S(1)}, bf...) custom-call(s32[2,64]{1,0:T(2,128)S(1)} %bitcast.1, ...), custom_call_target="tpu_custom_call" | custom-call | tf_op jit(solution)/shard_map/gather_looks/pallas_call | solution.py:404
  33.8 2.8 %filter_edges.1 = (f32[2,16,32,64]{3,2,1,0:T(8,128)}, f32[16,32,64]{2,1,0:T(8,128)}) custom-call(f32[2,32,1024]{2,1,0:T(8,128)S(1)} %get-tuple-element.13.edges_ref, f32[64,1024]{1,0:T(8,128)S(1)} %get-tuple-element.14.acc_ref, f32[16,32,64]{2,1,0:T(8,128)S(1)} %get-tuple-element.15.coh_in, bf16[64,96]{1,0:T(8,128)(2,1)S(1)} %get-tuple-element.16.refs_0_, ...), custom_call_target="tpu_custom_call" | custom-call | tf_op jit(solution)/shard_map/filter_edges/pallas_call | solution.py:439
Async XLA Ops:
  0.6 0.7 %copy-start.1 = (s32[64,2]{0,1:T(2,128)S(1)}, s32[64,2]{0,1:T(2,128)}, u32[]{:S(2)}) copy-start(s32[64,2]{0,1:T(2,128)} %param.3) | copy-start | bytes 1540
  1.3 1.1 %copy-start = (f32[6,2,64,256]{3,2,1,0:T(8,128)S(1)}, f32[6,2,64,256]{3,2,1,0:T(8,128)}, u32[]{:S(2)}) copy-start(f32[6,2,64,256]{3,2,1,0:T(8,128)} %slc_hbm.1) | copy-start | bytes 2359300

commit v4 on v3

--- a/solution.py
+++ b/solution.py
@@ -156,32 +156,23 @@
 
 
 def gather_kernel(
-    owners, tiles, pair_count, table_count, pairs_ref, slc_hbm, *refs
+    owners, tiles, pair_count, table_count, pairs_ref, slc_ref, *refs
 ):
     edges_ref, acc_ref, coh_ref = refs[:3]
     tables, refs = refs[3 : 3 + table_count], refs[3 + table_count :]
-    chunks = slc_hbm.shape[3] // LANES
-    slc_refs, recvs, refs = refs[:chunks], refs[chunks : 2 * chunks], refs[2 * chunks :]
+    chunks = slc_ref.shape[3] // LANES
+    recvs, refs = refs[:chunks], refs[chunks:]
     (
-        look_ref, look_t_ref, send, low_tab, prods, powers, natural,
+        look_ref, look_t_ref, send, low_tab, slots, prods, powers, natural,
         power_looked, looked, halo_low, halo_high,
-        load_sem, send_sem, recv_sem, halo_send_sem, halo_recv_sem,
+        send_sem, recv_sem, halo_send_sem, halo_recv_sem,
     ) = refs
     me = lax.axis_index("date")
     tile = lax.axis_index("tile")
-    dates_here, _, rows_here, _ = slc_hbm.shape
+    dates_here, _, rows_here, _ = slc_ref.shape
     half_rows = rows_here // AZ
     local_cols = chunks * LANES // RG
     chunk_cols = LANES // RG
-
-    loads = [
-        pltpu.make_async_copy(
-            slc_hbm.at[:, :, :, pl.ds(h * LANES, LANES)], slc_refs[h], load_sem.at[h]
-        )
-        for h in range(chunks)
-    ]
-    for load in loads:
-        load.start()
 
     barrier = pltpu.get_barrier_semaphore()
     for offset in range(1, owners):
@@ -216,7 +207,7 @@
     def stage(target, h, low, high):
         for rank, pick in ((0, low), (1, high)):
             for part in range(2):
-                target[rank, part] = slc_refs[h][pick, part]
+                target[rank, part] = slc_ref[pick, part, :, h * LANES : (h + 1) * LANES]
 
     def date_copy(h, offset, source, target):
         return pltpu.make_async_remote_copy(
@@ -228,15 +219,19 @@
             device_id_type=MESH,
         )
 
-    picks = [ends(lax.rem(me + offset, owners), me) for offset in range(1, owners)]
     below = lax.div(tile + tiles - 1, tiles)
     above = lax.div(2 * (tiles - 1) - tile, tiles)
-    pl.semaphore_wait(barrier, owners - 1 + below + above)
+    order = sorted(range(1, owners), key=lambda offset: abs(2 * offset - owners))
+    picks = {}
     for h in range(chunks):
-        loads[h].wait()
-        for offset in range(1, owners):
-            stage(send.at[h, offset - 1], h, *picks[offset - 1])
-            date_copy(h, offset, me, lax.rem(me + offset, owners)).start()
+        for offset in order:
+            target = lax.rem(me + offset, owners)
+            if h == 0:
+                picks[offset] = ends(target, me)
+            stage(send.at[h, offset - 1], h, *picks[offset])
+            if h == 0 and offset == order[0]:
+                pl.semaphore_wait(barrier, owners - 1 + below + above)
+            date_copy(h, offset, me, target).start()
 
     low, high = ends(me, me)
     for h in range(chunks):
@@ -247,11 +242,18 @@
     acc_ref[...] = jnp.zeros(acc_ref.shape, F32)
     fill_tables(look_ref, look_t_ref, *tables)
 
+    def find(i, _):
+        for c in range(2):
+            date = pairs_ref[c, me * pair_count + i]
+            source = lax.div(date, jnp.int32(dates_here))
+            slots[2 * c, i] = source
+            slots[2 * c + 1, i] = jnp.where(date == low_tab[source], 0, 1)
+        return 0
+
+    lax.fori_loop(0, pair_count, find, 0)
+
     def slot(i, c):
-        date = pairs_ref[c, me * pair_count + i]
-        source = lax.div(date, jnp.int32(dates_here))
-        rank = jnp.where(date == low_tab[source], 0, 1)
-        return source, rank
+        return slots[2 * c, i], slots[2 * c + 1, i]
 
     def halo_copy(up):
         step = 1 if up else -1
@@ -286,7 +288,7 @@
             prods[i, 1] = imag
             return 0
 
-        lax.fori_loop(0, pair_count, product, 0)
+        lax.fori_loop(0, pair_count, product, 0, unroll=4)
         high, low = split(prods[...].reshape(pair_count * 2 * half_rows, LANES))
         table = look_ref[...]
         looked[pl.ds(h * chunk_cols, chunk_cols)] = dot_nt(table, high) + dot_nt(table, low)
@@ -317,7 +319,7 @@
                 powers[i, rank] = total
             return 0
 
-        lax.fori_loop(0, owners, power, 0)
+        lax.fori_loop(0, owners, power, 0, unroll=2)
         high, low = split(powers[...].reshape(owners * REQ * half_rows, LANES))
         new = (dot(high, table) + dot(low, table)).reshape(power_looked.shape)
         power_looked[...] = new if h == 0 else power_looked[...] + new
@@ -335,7 +337,7 @@
         coh_ref[i] = (real * real + imag * imag) / (power_looked[sa, ra] * power_looked[sb, rb])
         return 0
 
-    lax.fori_loop(0, pair_count, coherence, 0)
+    lax.fori_loop(0, pair_count, coherence, 0, unroll=4)
     edges_ref[0, pl.ds(HALF, HALF)] = looked[pl.ds(0, HALF)]
     edges_ref[1, pl.ds(0, HALF)] = looked[pl.ds(local_cols - HALF, HALF)]
 
@@ -399,7 +401,6 @@
     lanes = pair_count * 2 * half_rows
     vmem = pl.BlockSpec(memory_space=pltpu.VMEM)
     smem = pl.BlockSpec(memory_space=pltpu.SMEM)
-    hbm = pl.BlockSpec(memory_space=pltpu.HBM)
     tables = [jax.ShapeDtypeStruct(shape, BF16) for shape in table_shapes()]
     outs = pl.pallas_call(
         functools.partial(gather_kernel, owners, tiles, pair_count, len(tables)),
@@ -409,15 +410,15 @@
             jax.ShapeDtypeStruct((pair_count, half_rows, looked_cols), F32),
             *tables,
         ),
-        in_specs=[smem, hbm],
+        in_specs=[smem, vmem],
         out_specs=(vmem,) * (3 + len(tables)),
         scratch_shapes=[
-            *[pltpu.VMEM((*slc.shape[:3], LANES), F32)] * chunks,
             *[pltpu.VMEM((owners, REQ, 2, rows, LANES), F32)] * chunks,
             pltpu.VMEM((LANES // RG, LANES), BF16),
             pltpu.VMEM((cols, looked_cols), BF16),
             pltpu.VMEM((chunks, owners - 1, REQ, 2, rows, LANES), F32),
             pltpu.SMEM((owners,), jnp.int32),
+            pltpu.SMEM((4, pair_count), jnp.int32),
             pltpu.VMEM((pair_count, 2, half_rows, LANES), F32),
             pltpu.VMEM((owners, REQ, half_rows, LANES), F32),
             pltpu.VMEM((pair_count, 2, half_rows, looked_cols), F32),
@@ -425,7 +426,6 @@
             pltpu.VMEM((looked_cols, lanes), F32),
             pltpu.VMEM((HALF, lanes), F32),
             pltpu.VMEM((HALF, lanes), F32),
-            pltpu.SemaphoreType.DMA((chunks,)),
             pltpu.SemaphoreType.DMA((chunks, owners - 1)),
             pltpu.SemaphoreType.DMA((chunks, owners)),
             pltpu.SemaphoreType.DMA((2,)),

time: 36.8 us -> 36 us (0.978)
  Pallas kernels: 34.1 us -> 33.4 us
    pallas_call x1, Pallas kernels: 31.3 us -> 30.6 us  [local(): pl.pallas_call(functools.partial(gather_kernel, owners, tiles, pair_count...]
where the time goes in v4:
time: 36 us; the launch traced here: 35.9 us
  Pallas kernels  33.4 us (93%)
  local copies, waits for them, and re-layouts  1.8 us (5%)
  between operations  0.65 us (2%)
    pallas_call x1, Pallas kernels, local(): pl.pallas_call(functools.partial(gather_kernel, owners, tiles, pair_count...  30.6 us
    pallas_call x1, Pallas kernels, local(): pl.pallas_call(filter_kernel, out_shape=(jax.ShapeDtypeStruct((2, pair_co...  2.79 us
    unnamed x4, local copies, waits for them, and re-layouts  1.8 us

profile of v4, /device:TPU:0, one launch (start us, length us, event | category | flops | bytes accessed | tf_op | source)
XLA Modules:
  0.0 35.9 jit_solution(16160789744023550570)
XLA Ops:
  0.6 0.0 copy-start.1
  0.6 0.7 %copy-done.1 = s32[64,2]{0,1:T(2,128)S(1)} copy-done((s32[64,2]{0,1:T(2,128)S(1)}, s32[64,2]{0,1:T(2,128)}, u32[]{:S(2)}) %copy-start.1) | copy-done | bytes 536
  1.3 0.0 copy-start
  1.3 1.1 %copy-done = f32[6,2,64,256]{3,2,1,0:T(8,128)S(1)} copy-done((f32[6,2,64,256]{3,2,1,0:T(8,128)S(1)}, f32[6,2,64,256]{3,2,1,0:T(8,128)}, u32[]{:S(2)}) %copy-start) | copy-done | bytes 786456
  2.4 30.6 %gather_looks.1 = (f32[2,32,1024]{2,1,0:T(8,128)S(1)}, f32[64,1024]{1,0:T(8,128)S(1)}, f32[16,32,64]{2,1,0:T(8,128)S(1)}, bf16[64,96]{1,0:T(8,128)(2,1)S(1)}, bf...) custom-call(s32[2,64]{1,0:T(2,128)S(1)} %bitcast.1, ...), custom_call_target="tpu_custom_call" | custom-call | tf_op jit(solution)/shard_map/gather_looks/pallas_call | solution.py:405
  33.1 2.8 %filter_edges.1 = (f32[2,16,32,64]{3,2,1,0:T(8,128)}, f32[16,32,64]{2,1,0:T(8,128)}) custom-call(f32[2,32,1024]{2,1,0:T(8,128)S(1)} %get-tuple-element.13.edges_ref, f32[64,1024]{1,0:T(8,128)S(1)} %get-tuple-element.14.acc_ref, f32[16,32,64]{2,1,0:T(8,128)S(1)} %get-tuple-element.15.coh_in, bf16[64,96]{1,0:T(8,128)(2,1)S(1)} %get-tuple-element.16.refs_0_, ...), custom_call_target="tpu_custom_call" | custom-call | tf_op jit(solution)/shard_map/filter_edges/pallas_call | solution.py:439
Async XLA Ops:
  0.6 0.7 %copy-start.1 = (s32[64,2]{0,1:T(2,128)S(1)}, s32[64,2]{0,1:T(2,128)}, u32[]{:S(2)}) copy-start(s32[64,2]{0,1:T(2,128)} %param.3) | copy-start | bytes 1540
  1.3 1.1 %copy-start = (f32[6,2,64,256]{3,2,1,0:T(8,128)S(1)}, f32[6,2,64,256]{3,2,1,0:T(8,128)}, u32[]{:S(2)}) copy-start(f32[6,2,64,256]{3,2,1,0:T(8,128)} %slc_ref.1) | copy-start | bytes 2359300

commit v5 on v4

--- a/solution.py
+++ b/solution.py
@@ -231,7 +231,8 @@
             stage(send.at[h, offset - 1], h, *picks[offset])
             if h == 0 and offset == order[0]:
                 pl.semaphore_wait(barrier, owners - 1 + below + above)
-            date_copy(h, offset, me, target).start()
+            if h == 0:
+                date_copy(h, offset, me, target).start()
 
     low, high = ends(me, me)
     for h in range(chunks):
@@ -254,6 +255,12 @@
 
     def slot(i, c):
         return slots[2 * c, i], slots[2 * c + 1, i]
+
+    for h in range(1, chunks):
+        for offset in order:
+            target = lax.rem(me + offset, owners)
+            date_copy(h - 1, offset, me, target).wait_send()
+            date_copy(h, offset, me, target).start()
 
     def halo_copy(up):
         step = 1 if up else -1
@@ -367,9 +374,8 @@
     def _():
         halo_copy(False).wait_send()
 
-    for h in range(chunks):
-        for offset in range(1, owners):
-            date_copy(h, offset, me, lax.rem(me + offset, owners)).wait_send()
+    for offset in range(1, owners):
+        date_copy(chunks - 1, offset, me, lax.rem(me + offset, owners)).wait_send()
 
 
 def filter_kernel(edges_ref, acc_ref, coh_in, *refs):

time: 36 us -> 36.3 us (level)
  no operation moved by 1% of the time
where the time goes in v5:
time: 36.3 us; the launch traced here: 36.1 us
  Pallas kernels  33.6 us (93%)
  local copies, waits for them, and re-layouts  1.8 us (5%)
  between operations  0.65 us (2%)
    pallas_call x1, Pallas kernels, local(): pl.pallas_call(functools.partial(gather_kernel, owners, tiles, pair_count...  30.8 us
    pallas_call x1, Pallas kernels, local(): pl.pallas_call(filter_kernel, out_shape=(jax.ShapeDtypeStruct((2, pair_co...  2.79 us
    unnamed x4, local copies, waits for them, and re-layouts  1.8 us

profile of v5, /device:TPU:0, one launch (start us, length us, event | category | flops | bytes accessed | tf_op | source)
XLA Modules:
  0.0 36.1 jit_solution(5235305044660719024)
XLA Ops:
  0.6 0.0 copy-start.1
  0.6 0.7 %copy-done.1 = s32[64,2]{0,1:T(2,128)S(1)} copy-done((s32[64,2]{0,1:T(2,128)S(1)}, s32[64,2]{0,1:T(2,128)}, u32[]{:S(2)}) %copy-start.1) | copy-done | bytes 536
  1.3 0.0 copy-start
  1.3 1.1 %copy-done = f32[6,2,64,256]{3,2,1,0:T(8,128)S(1)} copy-done((f32[6,2,64,256]{3,2,1,0:T(8,128)S(1)}, f32[6,2,64,256]{3,2,1,0:T(8,128)}, u32[]{:S(2)}) %copy-start) | copy-done | bytes 786456
  2.4 30.8 %gather_looks.1 = (f32[2,32,1024]{2,1,0:T(8,128)S(1)}, f32[64,1024]{1,0:T(8,128)S(1)}, f32[16,32,64]{2,1,0:T(8,128)S(1)}, bf16[64,96]{1,0:T(8,128)(2,1)S(1)}, bf...) custom-call(s32[2,64]{1,0:T(2,128)S(1)} %bitcast.1, ...), custom_call_target="tpu_custom_call" | custom-call | tf_op jit(solution)/shard_map/gather_looks/pallas_call | solution.py:411
  33.3 2.8 %filter_edges.1 = (f32[2,16,32,64]{3,2,1,0:T(8,128)}, f32[16,32,64]{2,1,0:T(8,128)}) custom-call(f32[2,32,1024]{2,1,0:T(8,128)S(1)} %get-tuple-element.13.edges_ref, f32[64,1024]{1,0:T(8,128)S(1)} %get-tuple-element.14.acc_ref, f32[16,32,64]{2,1,0:T(8,128)S(1)} %get-tuple-element.15.coh_in, bf16[64,96]{1,0:T(8,128)(2,1)S(1)} %get-tuple-element.16.refs_0_, ...), custom_call_target="tpu_custom_call" | custom-call | tf_op jit(solution)/shard_map/filter_edges/pallas_call | solution.py:445
Async XLA Ops:
  0.6 0.7 %copy-start.1 = (s32[64,2]{0,1:T(2,128)S(1)}, s32[64,2]{0,1:T(2,128)}, u32[]{:S(2)}) copy-start(s32[64,2]{0,1:T(2,128)} %param.3) | copy-start | bytes 1540
  1.3 1.1 %copy-start = (f32[6,2,64,256]{3,2,1,0:T(8,128)S(1)}, f32[6,2,64,256]{3,2,1,0:T(8,128)}, u32[]{:S(2)}) copy-start(f32[6,2,64,256]{3,2,1,0:T(8,128)} %slc_ref.1) | copy-start | bytes 2359300

commit v6 on v4

--- a/solution.py
+++ b/solution.py
@@ -326,6 +326,10 @@
 
         per_chunk = chunk_cols // HALF
         inner = [k for k in range(h * per_chunk, (h + 1) * per_chunk) if k > 0]
+        if h == chunks - 1:
+            for n, k in enumerate(inner):
+                edges_ref[2 + n] = looked[pl.ds((k - 1) * HALF, PATCH)]
+            continue
         results = filtered([looked[pl.ds((k - 1) * HALF, PATCH)] for k in inner], tables)
         for k, result in zip(inner, results):
             acc_ref[pl.ds((k - 1) * HALF, PATCH)] += result
@@ -375,15 +379,16 @@
 def filter_kernel(edges_ref, acc_ref, coh_in, *refs):
     tables, (out_ref, coh_out) = refs[:-2], refs[-2:]
     coh_out[...] = coh_in[...]
-    first, last = filtered([edges_ref[0], edges_ref[1]], tables)
-    final = jnp.concatenate(
-        [
-            acc_ref[:HALF] + first[HALF:],
-            acc_ref[HALF:-HALF],
-            acc_ref[-HALF:] + last[:HALF],
-        ],
-        axis=0,
-    ).T
+    count = acc_ref.shape[0] // HALF
+    sums = [acc_ref[b * HALF : (b + 1) * HALF] for b in range(count)]
+    fields = [edges_ref[n] for n in range(edges_ref.shape[0])]
+    late = len(fields) - 2
+    for k, result in zip((0, count, *range(count - late, count)), filtered(fields, tables)):
+        if k > 0:
+            sums[k - 1] = sums[k - 1] + result[:HALF]
+        if k < count:
+            sums[k] = sums[k] + result[HALF:]
+    final = jnp.concatenate(sums, axis=0).T
     for p in range(out_ref.shape[1]):
         for c in range(2):
             at = (p * 2 + c) * PATCH
@@ -399,13 +404,14 @@
     chunks = cols // LANES
     pair_count = pairs.shape[0] // owners
     lanes = pair_count * 2 * half_rows
+    late = LANES // RG // HALF - (chunks == 1)
     vmem = pl.BlockSpec(memory_space=pltpu.VMEM)
     smem = pl.BlockSpec(memory_space=pltpu.SMEM)
     tables = [jax.ShapeDtypeStruct(shape, BF16) for shape in table_shapes()]
     outs = pl.pallas_call(
         functools.partial(gather_kernel, owners, tiles, pair_count, len(tables)),
         out_shape=(
-            jax.ShapeDtypeStruct((2, PATCH, lanes), F32),
+            jax.ShapeDtypeStruct((2 + late, PATCH, lanes), F32),
             jax.ShapeDtypeStruct((looked_cols, lanes), F32),
             jax.ShapeDtypeStruct((pair_count, half_rows, looked_cols), F32),
             *tables,

time: 36 us -> 36 us (level); the launches traced: 35.9 us -> 35.2 us
  Pallas kernels: 33.4 us -> 32.8 us
    pallas_call x1, Pallas kernels: 30.6 us -> 29 us  [local(): pl.pallas_call(functools.partial(gather_kernel, owners, tiles, pair_count...]
    pallas_call x1, Pallas kernels: 2.79 us -> 3.84 us  [local(): pl.pallas_call(filter_kernel, out_shape=(jax.ShapeDtypeStruct((2, pair_co...]
where the time goes in v6:
time: 36 us; the launch traced here: 35.2 us
  Pallas kernels  32.8 us (91%)
  local copies, waits for them, and re-layouts  1.8 us (5%)
  between operations  0.65 us (2%)
    pallas_call x1, Pallas kernels, local(): pl.pallas_call(functools.partial(gather_kernel, owners, tiles, pair_count...  29 us
    pallas_call x1, Pallas kernels, local(): pl.pallas_call(filter_kernel, out_shape=(jax.ShapeDtypeStruct((2, pair_co...  3.84 us
    unnamed x4, local copies, waits for them, and re-layouts  1.8 us

profile of v6, /device:TPU:0, one launch (start us, length us, event | category | flops | bytes accessed | tf_op | source)
XLA Modules:
  0.0 35.2 jit_solution(5316882180457688217)
XLA Ops:
  0.6 0.0 copy-start.1
  0.6 0.7 %copy-done.1 = s32[64,2]{0,1:T(2,128)S(1)} copy-done((s32[64,2]{0,1:T(2,128)S(1)}, s32[64,2]{0,1:T(2,128)}, u32[]{:S(2)}) %copy-start.1) | copy-done | bytes 536
  1.3 0.0 copy-start
  1.3 1.1 %copy-done = f32[6,2,64,256]{3,2,1,0:T(8,128)S(1)} copy-done((f32[6,2,64,256]{3,2,1,0:T(8,128)S(1)}, f32[6,2,64,256]{3,2,1,0:T(8,128)}, u32[]{:S(2)}) %copy-start) | copy-done | bytes 786456
  2.4 29.0 %gather_looks.1 = (f32[4,32,1024]{2,1,0:T(8,128)S(1)}, f32[64,1024]{1,0:T(8,128)S(1)}, f32[16,32,64]{2,1,0:T(8,128)S(1)}, bf16[64,96]{1,0:T(8,128)(2,1)S(1)}, bf...) custom-call(s32[2,64]{1,0:T(2,128)S(1)} %bitcast.1, ...), custom_call_target="tpu_custom_call" | custom-call | tf_op jit(solution)/shard_map/gather_looks/pallas_call | solution.py:411
  31.4 3.8 %filter_edges.1 = (f32[2,16,32,64]{3,2,1,0:T(8,128)}, f32[16,32,64]{2,1,0:T(8,128)}) custom-call(f32[4,32,1024]{2,1,0:T(8,128)S(1)} %get-tuple-element.13.edges_ref, f32[64,1024]{1,0:T(8,128)S(1)} %get-tuple-element.14.acc_ref, f32[16,32,64]{2,1,0:T(8,128)S(1)} %get-tuple-element.15.coh_in, bf16[64,96]{1,0:T(8,128)(2,1)S(1)} %get-tuple-element.16.refs_0_, ...), custom_call_target="tpu_custom_call" | custom-call | tf_op jit(solution)/shard_map/filter_edges/pallas_call | solution.py:445
Async XLA Ops:
  0.6 0.7 %copy-start.1 = (s32[64,2]{0,1:T(2,128)S(1)}, s32[64,2]{0,1:T(2,128)}, u32[]{:S(2)}) copy-start(s32[64,2]{0,1:T(2,128)} %param.3) | copy-start | bytes 1540
  1.3 1.1 %copy-start = (f32[6,2,64,256]{3,2,1,0:T(8,128)S(1)}, f32[6,2,64,256]{3,2,1,0:T(8,128)}, u32[]{:S(2)}) copy-start(f32[6,2,64,256]{3,2,1,0:T(8,128)} %slc_ref.1) | copy-start | bytes 2359300
